TPU v7x, 128 devices: a whole 4x4x4 slice. The times are simulated.
128 devices in a mesh: tm: 4 (over z), height: 16 (over x, y), width: 2 (over core).
Axes of the slice: x: 4, y: 4, z: 4, core: 2. Of those that a mesh axis runs over, the one named last changes fastest.
Arguments:
- latent: bfloat16 [128, 8, 64, 512], P(None, 'tm', 'height', 'width'), may hold values from -64 to 64
- exponents: int32 [32], replicated, may hold values from -1 to 1
- cotangent: bfloat16 [128, 8, 64, 512], P(None, 'tm', 'height', 'width'), may hold values from -6 to 6
- conv_first: bfloat16 [128, 3456], replicated, may hold values from -0.109375 to 0.109375
- conv_second: bfloat16 [128, 3456], replicated, may hold values from -0.109375 to 0.109375
- gain_first: float32 [128], replicated, may hold values from 0.1 to 1.9
- shift_first: float32 [128], replicated, may hold values from -2.5 to 2.5
- gain_second: float32 [128], replicated, may hold values from 0.1 to 1.9
- shift_second: float32 [128], replicated, may hold values from -2.5 to 2.5
Outputs:
- decoded_grad: float32 [128, 8, 64, 512], P(None, 'tm', 'height', 'width')
- conv_first_grad: float32 [128, 3456], replicated
- conv_second_grad: float32 [128, 3456], replicated
All inputs are finite; a program needn't handle non-finite values.
Results may differ from a plain program's by a relative error of at most 0.005.
Values may be sent and summed in bfloat16 or wider, within the bound.
A program may use at most 128 MiB of HBM per device.

v0:
```python
import jax
import jax.numpy as jnp
from jax import lax
from jax.sharding import PartitionSpec as P

epsilon = 1e-05


def padded_2(cells, sides, width):
    for axis, dim in sides:
        count = lax.axis_size(axis)
        ends = count - 1
        head = lax.slice_in_dim(cells, 0, width, axis=dim)
        tail = lax.slice_in_dim(cells, cells.shape[dim] - width, cells.shape[dim], axis=dim)
        cells = jnp.concatenate(
            [
                lax.ppermute(tail, axis, [(i, (i + 1) % count) for i in range(ends)]),
                cells,
                lax.ppermute(head, axis, [((i + 1) % count, i) for i in range(ends)]),
            ],
            axis=dim,
        )
    return cells


def from_behind(value, axis, steps):
    count = lax.axis_size(axis)
    initial, last = (max(0, -steps), min(count, count - steps))
    return lax.ppermute(value, axis, [(source, source + steps) for source in range(initial, last)])


def group_terms(values, groups):
    return jnp.sum(values.reshape(groups, -1), axis=1)


def per_channel(stat, channels):
    return jnp.repeat(stat, channels // stat.shape[0])[:, None, None, None]


def channel(vector):
    return vector[:, None, None, None]


def across(terms):
    return lax.psum(terms, ("tm", "height", "width"))


def group_stats(values, groups, count):
    channels = values.shape[0]
    (sums,) = across((group_terms(values, groups),))
    mean_value = sums / count
    centered = values - per_channel(mean_value, channels)
    (squares,) = across((group_terms(centered * centered, groups),))
    variance = squares / count
    inverse = 1.0 / jnp.sqrt(variance + epsilon)
    return (centered * per_channel(inverse, channels), inverse)


def silu_slope(pre):
    sigmoid_value = jax.nn.sigmoid(pre)
    return sigmoid_value * (1.0 + pre * (1.0 - sigmoid_value))


def norm_backward(grad, pre, normed, gain, inverse, groups, count):
    channels = grad.shape[0]
    scaled = grad * silu_slope(pre) * channel(gain)
    first_sum, second_sum = across(
        (group_terms(scaled, groups), group_terms(scaled * normed, groups))
    )
    return per_channel(inverse, channels) * (
        scaled
        - per_channel(first_sum / count, channels)
        - normed * per_channel(second_sum / count, channels)
    )


def rimmed(timed):
    return padded_2(timed, (("height", 2), ("width", 3)), 1)


def extend_past(values):
    before = from_behind(values, "tm", 1)
    return rimmed(jnp.concatenate([before, values], axis=1))


def extend_future(values):
    after = from_behind(values, "tm", -1)
    return rimmed(jnp.concatenate([values, after], axis=1))


def tap_stack(padded, first, top, col_taps, frame_count, row_count, col_count):
    pieces = [
        padded[:, first : first + frame_count, top : top + row_count, col_tap : col_tap + col_count]
        for col_tap in col_taps
    ]
    return jnp.concatenate(pieces, axis=0).reshape(len(col_taps) * padded.shape[0], -1)


def forward_conv(padded, weight, frame_count, row_count, col_count):
    channels = weight.shape[0]
    accum = jnp.zeros((channels, frame_count * row_count * col_count), jnp.float32)
    for depth_tap in range(3):
        for row_tap in range(3):
            start_col = (depth_tap * 3 + row_tap) * 3 * channels
            stacked = tap_stack(
                padded, depth_tap, row_tap, (0, 1, 2), frame_count, row_count, col_count
            )
            accum = accum + jnp.dot(
                weight[:, start_col : start_col + 3 * channels],
                stacked,
                preferred_element_type=jnp.float32,
            )
    return accum.reshape(channels, frame_count, row_count, col_count)


def transposed_conv(padded, weight, frame_count, row_count, col_count):
    channels = weight.shape[0]
    accum = jnp.zeros((channels, frame_count * row_count * col_count), jnp.float32)
    for depth_tap in range(3):
        for row_tap in range(3):
            start_col = (depth_tap * 3 + row_tap) * 3 * channels
            w_block = (
                weight[:, start_col : start_col + 3 * channels]
                .reshape(channels, 3, channels)
                .transpose(2, 1, 0)
                .reshape(channels, 3 * channels)
            )
            stacked = tap_stack(
                padded, 2 - depth_tap, 2 - row_tap, (2, 1, 0), frame_count, row_count, col_count
            )
            accum = accum + jnp.dot(w_block, stacked, preferred_element_type=jnp.float32)
    return accum.reshape(channels, frame_count, row_count, col_count)


def weight_terms(padded, grad, frame_count, row_count, col_count):
    channels = grad.shape[0]
    flat_grad = grad.reshape(channels, -1)
    pieces = []
    for depth_tap in range(3):
        for row_tap in range(3):
            stacked = tap_stack(
                padded, depth_tap, row_tap, (0, 1, 2), frame_count, row_count, col_count
            )
            pieces.append(
                lax.dot_general(
                    flat_grad, stacked, (((1,), (1,)), ((), ())), preferred_element_type=jnp.float32
                )
            )
    return jnp.concatenate(pieces, axis=1)


def reduce_weights(terms):
    result = lax.psum(terms, ("tm", "height", "width"))
    return result


def shards(
    latent,
    exponents,
    cotangent,
    conv_first,
    conv_second,
    gain_first,
    shift_first,
    gain_second,
    shift_second,
):
    channels, frame_count, row_count, col_count = latent.shape
    groups = exponents.shape[0]
    count = float(
        channels
        // groups
        * frame_count
        * row_count
        * col_count
        * lax.axis_size("tm")
        * lax.axis_size("height")
        * lax.axis_size("width")
    )
    decoded = latent.astype(jnp.float32) * per_channel(
        jnp.exp2(exponents.astype(jnp.float32)), channels
    )
    normed_first, inverse_first = group_stats(decoded, groups, count)
    pre_first = normed_first * channel(gain_first) + channel(shift_first)
    act_first = jax.nn.silu(pre_first).astype(jnp.bfloat16)
    padded_first = extend_past(act_first)
    hidden = forward_conv(padded_first, conv_first, frame_count, row_count, col_count)
    normed_second, inverse_second = group_stats(hidden, groups, count)
    pre_second = normed_second * channel(gain_second) + channel(shift_second)
    act_second = jax.nn.silu(pre_second).astype(jnp.bfloat16)
    padded_second = extend_past(act_second)
    padded_cotangent = extend_future(cotangent)
    grad_second = transposed_conv(padded_cotangent, conv_second, frame_count, row_count, col_count)
    conv_second_grad = reduce_weights(
        weight_terms(padded_second, cotangent, frame_count, row_count, col_count)
    )
    hidden_grad = norm_backward(
        grad_second, pre_second, normed_second, gain_second, inverse_second, groups, count
    ).astype(jnp.bfloat16)
    padded_hidden = extend_future(hidden_grad)
    grad_first = transposed_conv(padded_hidden, conv_first, frame_count, row_count, col_count)
    conv_first_grad = reduce_weights(
        weight_terms(padded_first, hidden_grad, frame_count, row_count, col_count)
    )
    decoded_grad = cotangent.astype(jnp.float32) + norm_backward(
        grad_first, pre_first, normed_first, gain_first, inverse_first, groups, count
    )
    return (decoded_grad, conv_first_grad, conv_second_grad)


def solution(mesh):
    placed = (
        P(None, "tm", "height", "width"),
        P(),
        P(None, "tm", "height", "width"),
        P(),
        P(),
        P(),
        P(),
        P(),
        P(),
    )
    return jax.shard_map(
        shards,
        mesh=mesh,
        in_specs=placed,
        out_specs=(P(None, "tm", "height", "width"), P(), P()),
        check_vma=False,
    )
```

profile of v0, /device:TPU:1, one launch (start us, length us, event | category | flops | bytes accessed | tf_op | source)
XLA Modules:
  0.0 786.0 jit_solution(15104056766058537244)
XLA Ops:
  11.2 68.7 %psum.70 = f32[32]{0:T(128)S(1)} all-reduce(f32[32]{0:T(128)S(1)} %reduce_sum.97), channel_id=1, replica_groups=mesh['tm'=4,'height'=16,'width'=2] {'tm','height','width'}, use_global_device_ids=true, to_apply=%region_2.0 | all-reduce | flops 32 | bytes 256 | tf_op jit(solution)/shard_map/psum | solution.py:45
  82.0 68.5 %psum.71 = f32[32]{0:T(128)S(1)} all-reduce(f32[32]{0:T(128)S(1)} %reduce_sum.100), channel_id=1, replica_groups=mesh['tm'=4,'height'=16,'width'=2] {'tm','height','width'}, use_global_device_ids=true, to_apply=%region_5.6 | all-reduce | flops 32 | bytes 256 | tf_op jit(solution)/shard_map/psum | solution.py:45
  151.5 2.7 collective-permute-start
  167.5 2.2 collective-permute-start.6
  172.8 4.7 collective-permute-start.1
  192.8 4.0 collective-permute-start.8
  203.7 3.2 collective-permute-start.4
  208.2 1.7 fusion.171
  211.5 3.5 maximum_maximum_fusion
  215.0 4.5 fusion.160
  220.6 1.6 copy.209
  226.7 1.6 copy.203
  229.8 1.6 copy.199
  232.8 1.6 copy.197
  234.4 3.4 pad_maximum_fusion.15
  237.9 2.6 copy.195
  240.5 2.6 pad_maximum_fusion.9
  243.1 2.6 copy.193
  245.6 3.0 fusion.143
  250.2 2.6 copy.207
  252.7 2.5 convolution_add_fusion.23
  263.7 2.1 fusion.177
  267.2 2.6 maximum_maximum_fusion.5
  269.8 67.8 %psum.72 = f32[32]{0:T(128)S(1)} all-reduce(f32[32]{0:T(128)S(1)} %copy-done.129), channel_id=1, replica_groups=mesh['tm'=4,'height'=16,'width'=2] {'tm','height','width'}, use_global_device_ids=true, to_apply=%region_8.9 | all-reduce | flops 32 | bytes 256 | tf_op jit(solution)/shard_map/psum | solution.py:45
  338.4 2.0 multiply_reduce_fusion.2
  341.8 3.5 fusion.173
  345.4 63.2 %psum.73 = f32[32]{0:T(128)S(1)} all-reduce(f32[32]{0:T(128)S(1)} %copy-done.128), channel_id=1, replica_groups=mesh['tm'=4,'height'=16,'width'=2] {'tm','height','width'}, use_global_device_ids=true, to_apply=%region_11.12 | all-reduce | flops 32 | bytes 256 | tf_op jit(solution)/shard_map/psum | solution.py:45
  409.3 2.4 pad_maximum_fusion.3
  411.8 2.3 fusion.162
  425.9 1.9 fusion.155
  428.2 2.5 copy.243
  430.7 63.1 %all-reduce.1 = (f32[32]{0:T(128)S(1)}, f32[32]{0:T(128)S(1)}) all-reduce(f32[32]{0:T(128)S(1)} %reduce_sum.145, f32[32]{0:T(128)S(1)} %reduce_sum.115), channel_id=1, replica_groups=mesh['tm'=4,'height'=16,'width'=2] {'tm','height','width'}, use_global_device_ids=true, to_apply=%region_17.18 | all-reduce | flops 64 | bytes 512 | tf_op jit(solution)/shard_map/psum | solution.py:45
  495.5 2.7 multiply_convert_fusion
  500.2 4.2 collective-permute-start.15
  511.5 3.1 collective-permute-done.15
  514.7 2.4 collective-permute-start.16
  520.7 4.0 collective-permute-start.11
  532.6 5.3 collective-permute-start.19
  549.7 1.9 copy.270
  551.6 4.6 maximum_maximum_fusion.2
  556.2 2.2 fusion.156
  558.4 3.6 fusion.157
  563.7 4.6 pad_maximum_fusion.1
  568.3 3.2 fusion.158
  571.5 2.0 fusion.159
  574.8 2.6 copy.260
  577.4 2.6 pad_maximum_fusion.30
  580.0 2.6 copy.258
  582.6 2.6 pad_maximum_fusion.29
  585.2 2.6 copy.254
  587.8 2.6 pad_maximum_fusion.28
  590.4 2.7 copy.252
  593.1 3.6 pad_maximum_fusion.32
  596.7 2.7 copy.250
  600.7 1.6 copy.248
  602.2 2.2 copy.256
  604.5 2.7 fusion.103
  628.9 1.9 copy.262
  630.7 1.8 convolution_add_fusion.1
  634.6 2.1 fusion.154
  637.2 70.7 %all-reduce = (f32[32]{0:T(128)S(1)}, f32[32]{0:T(128)S(1)}) all-reduce(f32[32]{0:T(128)S(1)} %reduce_sum.151, f32[32]{0:T(128)S(1)} %reduce_sum.148), channel_id=1, replica_groups=mesh['tm'=4,'height'=16,'width'=2] {'tm','height','width'}, use_global_device_ids=true, to_apply=%region_23.24 | all-reduce | flops 64 | bytes 512 | tf_op jit(solution)/shard_map/psum | solution.py:45
  708.7 1.6 copy.280
  710.4 64.3 %all-reduce.5.cloned.1.call-done = (f32[128,3456]{1,0:T(8,128)}, f32[128,3456]{0,1:T(8,128)}) async-done(((f32[128,3456]{1,0:T(8,128)}, f32[128,3456]{0,1:T(8,128)}), (f32[128,3456]{1,0:T(8,128)}, f32[128,3456]{0,1:T(8,128)})) %all-reduce.5.cloned.1.call-update) | async-done | bytes 3538960 | tf_op jit(solution)/shard_map/psum | solution.py:153
  774.7 2.8 copy.281
  (475 shorter events, 146.8 us)
Async XLA Ops:
  7.2 73.0 %copy-start = (bf16[128,2,4,256]{3,2,1,0:T(4,128)(2,1)S(1)}, bf16[128,2,4,256]{3,2,1,0:T(4,128)(2,1)}, u32[]{:S(2)}) copy-start(bf16[128,2,4,256]{3,2,1,0:T(4,128)(2,1)} %param.9) | copy-start | bytes 1572868
  7.2 143.6 %copy-start.123 = (f32[128]{0:T(128)S(1)}, f32[128]{0:T(128)}, u32[]{:S(2)}) copy-start(f32[128]{0:T(128)} %param.14) | copy-start | bytes 1540
  7.2 143.5 %copy-start.121 = (f32[128]{0:T(128)S(1)}, f32[128]{0:T(128)}, u32[]{:S(2)}) copy-start(f32[128]{0:T(128)} %param.15) | copy-start | bytes 1540
  7.2 767.5 %all-reduce.5.cloned.1.call-start = ((), (), s32[]{:S(2)}) async-start(), calls=%async_computation | async-start | bytes 7077888 | tf_op jit(solution)/shard_map/psum | solution.py:153
  8.1 143.4 %copy-start.114 = (f32[128]{0:T(128)}, f32[128]{0:T(128)S(1)}, u32[]{:S(2)}) copy-start(f32[128]{0:T(128)S(1)} %mul.184) | copy-start | bytes 1540
  8.1 146.1 %copy-start.75 = (bf16[128,3456]{1,0:T(8,128)(2,1)S(1)}, bf16[128,3456]{1,0:T(8,128)(2,1)}, u32[]{:S(2)}) copy-start(bf16[128,3456]{1,0:T(8,128)(2,1)} %param.13) | copy-start | bytes 2654212
  80.1 71.4 %copy-start.116 = (f32[128]{0:T(128)}, f32[128]{0:T(128)S(1)}, u32[]{:S(2)}) copy-start(f32[128]{0:T(128)S(1)} %sub.72) | copy-start | bytes 1540
  80.7 85.9 %collective-permute-start.5 = (bf16[128,2,4,256]{0,3,2,1:T(8,128)(2,1)S(1)}, bf16[128,2,4,256]{0,3,2,1:T(8,128)(2,1)S(1)}, u32[]{:S(2)}, u32[]{:S(2)}) collective-permute-start(bf16[128,2,4,256]{0,3,2,1:T(8,128)(2,1)S(1)} %copy.212), channel_id=1, source_target_pairs={{32,0},{64,32},{96,64},{33,1},{65,33},{97,65},{34,2},{66,34},{98,6... | collective-permute-start | bytes 1572872 | tf_op jit(solution)/shard_map/ppermute | solution.py:29
  151.5 20.3 %collective-permute-start = (bf16[128,2,4,256]{3,0,2,1:T(8,128)(2,1)S(1)}, bf16[128,2,4,256]{3,0,2,1:T(8,128)(2,1)S(1)}, u32[]{:S(2)}, u32[]{:S(2)}) collective-permute-start(bf16[128,2,4,256]{3,0,2,1:T(8,128)(2,1)S(1)} %multiply_convert_fusion.2), channel_id=1, source_target_pairs={{0,32},{32,64},{64,96},{1,33},{33,65},{65,97},{2,34},{34,66},{66,9... | collective-permute-start | bytes 1572872 | tf_op jit(solution)/shard_map/ppermute | solution.py:29
  166.6 12.1 %copy-start.25 = (bf16[128,3456]{1,0:T(8,128)(2,1)S(1)}, bf16[128,3456]{1,0:T(8,128)(2,1)}, u32[]{:S(2)}) copy-start(bf16[128,3456]{1,0:T(8,128)(2,1)} %param.12) | copy-start | bytes 2654212
  167.5 22.9 %collective-permute-start.6 = (bf16[128,4,1,256]{3,0,2,1:T(8,128)(2,1)}, bf16[128,4,1,256]{3,0,2,1:T(8,128)(2,1)}, u32[]{:S(2)}, u32[]{:S(2)}) collective-permute-start(bf16[128,4,1,256]{3,0,2,1:T(8,128)(2,1)} %copy.213), channel_id=1, source_target_pairs={{0,2},{2,4},{4,6},{6,8},{8,10},{10,12},{12,14},{14,16},{16,18},{18... | collective-permute-start | bytes 786440 | tf_op jit(solution)/shard_map/ppermute | solution.py:17
  170.6 21.0 %collective-permute-start.7 = (bf16[128,4,1,256]{3,0,2,1:T(8,128)(2,1)}, bf16[128,4,1,256]{3,0,2,1:T(8,128)(2,1)}, u32[]{:S(2)}, u32[]{:S(2)}) collective-permute-start(bf16[128,4,1,256]{3,0,2,1:T(8,128)(2,1)} %copy.214), channel_id=1, source_target_pairs={{2,0},{4,2},{6,4},{8,6},{10,8},{12,10},{14,12},{16,14},{18,16},{20... | collective-permute-start | bytes 786440 | tf_op jit(solution)/shard_map/ppermute | solution.py:19
  171.9 39.6 %copy-start.2 = (bf16[128,2,4,256]{3,0,2,1:T(8,128)(2,1)}, bf16[128,2,4,256]{3,0,2,1:T(8,128)(2,1)S(1)}, u32[]{:S(2)}) copy-start(bf16[128,2,4,256]{3,0,2,1:T(8,128)(2,1)S(1)} %collective-permute-done) | copy-start | bytes 1572868
  172.8 25.3 %collective-permute-start.1 = (bf16[128,4,1,256]{3,0,2,1:T(8,128)(2,1)}, bf16[128,4,1,256]{3,0,2,1:T(8,128)(2,1)}, u32[]{:S(2)}, u32[]{:S(2)}) collective-permute-start(bf16[128,4,1,256]{3,0,2,1:T(8,128)(2,1)} %get-tuple-element.150), channel_id=1, source_target_pairs={{0,2},{2,4},{4,6},{6,8},{8,10},{10,12},{12,14},{14,16},{16,18},{18... | collective-permute-start | bytes 786440 | tf_op jit(solution)/shard_map/ppermute | solution.py:17
  177.5 20.6 %collective-permute-start.2 = (bf16[128,4,1,256]{3,0,2,1:T(8,128)(2,1)}, bf16[128,4,1,256]{3,0,2,1:T(8,128)(2,1)}, u32[]{:S(2)}, u32[]{:S(2)}) collective-permute-start(bf16[128,4,1,256]{3,0,2,1:T(8,128)(2,1)} %get-tuple-element.151), channel_id=1, source_target_pairs={{2,0},{4,2},{6,4},{8,6},{10,8},{12,10},{14,12},{16,14},{18,16},{20... | collective-permute-start | bytes 786440 | tf_op jit(solution)/shard_map/ppermute | solution.py:19
  192.7 6.7 copy-start.24
  192.8 216.5 %collective-permute-start.8 = (bf16[128,4,6,1]{0,1,3,2:T(4,128)(2,1)S(1)}, bf16[128,4,6,1]{0,1,3,2:T(4,128)(2,1)S(1)}, u32[]{:S(2)}, u32[]{:S(2)}) collective-permute-start(bf16[128,4,6,1]{0,1,3,2:T(4,128)(2,1)S(1)} %copy.217), channel_id=1, source_target_pairs={{1,0},{3,2},{5,4},{7,6},{9,8},{11,10},{13,12},{15,14},{17,16},{19,... | collective-permute-start | bytes 18440 | tf_op jit(solution)/shard_map/ppermute | solution.py:19
  196.8 212.5 %collective-permute-start.9 = (bf16[128,4,6,1]{0,1,3,2:T(4,128)(2,1)S(1)}, bf16[128,4,6,1]{0,1,3,2:T(4,128)(2,1)S(1)}, u32[]{:S(2)}, u32[]{:S(2)}) collective-permute-start(bf16[128,4,6,1]{0,1,3,2:T(4,128)(2,1)S(1)} %copy.220), channel_id=1, source_target_pairs={{0,1},{2,3},{4,5},{6,7},{8,9},{10,11},{12,13},{14,15},{16,17},{18,... | collective-permute-start | bytes 18440 | tf_op jit(solution)/shard_map/ppermute | solution.py:17
  202.1 7.7 collective-permute-start.3
  203.7 6.6 collective-permute-start.4
  215.0 5.5 copy-start.39
  252.7 2.5 copy-start.19
  252.7 2.5 copy-start.26
  267.2 2.6 copy-start.129
  341.8 3.5 copy-start.128
  411.8 2.3 copy-start.67
  495.5 2.7 copy-start.49
  495.5 2.7 copy-start.58
  495.5 2.7 copy-start.59
  498.2 29.3 %copy-start.4 = (bf16[128,2,4,256]{3,0,2,1:T(8,128)(2,1)}, bf16[128,2,4,256]{3,0,2,1:T(8,128)(2,1)S(1)}, u32[]{:S(2)}) copy-start(bf16[128,2,4,256]{3,0,2,1:T(8,128)(2,1)S(1)} %get-tuple-element.138) | copy-start | bytes 1572868
  498.2 6.1 copy-start.3
  498.2 6.1 copy-start.37
  498.2 6.1 copy-start.38
  498.9 20.1 %collective-permute-start.10 = (bf16[128,2,4,256]{3,0,2,1:T(8,128)(2,1)S(1)}, bf16[128,2,4,256]{3,0,2,1:T(8,128)(2,1)S(1)}, u32[]{:S(2)}, u32[]{:S(2)}) collective-permute-start(bf16[128,2,4,256]{3,0,2,1:T(8,128)(2,1)S(1)} %get-tuple-element.139), channel_id=1, source_target_pairs={{32,0},{64,32},{96,64},{33,1},{65,33},{97,65},{34,2},{66,34},{98,6... | collective-permute-start | bytes 1572872 | tf_op jit(solution)/shard_map/ppermute | solution.py:29
  500.2 4.8 copy-start.44
  500.2 4.8 copy-start.56
  500.2 4.8 copy-start.57
  500.2 14.4 %collective-permute-start.15 = (bf16[128,2,4,256]{3,0,2,1:T(8,128)(2,1)S(1)}, bf16[128,2,4,256]{3,0,2,1:T(8,128)(2,1)S(1)}, u32[]{:S(2)}, u32[]{:S(2)}) collective-permute-start(bf16[128,2,4,256]{3,0,2,1:T(8,128)(2,1)S(1)} %get-tuple-element.138), channel_id=1, source_target_pairs={{0,32},{32,64},{64,96},{1,33},{33,65},{65,97},{2,34},{34,66},{66,9... | collective-permute-start | bytes 1572872 | tf_op jit(solution)/shard_map/ppermute | solution.py:29
  510.9 7.4 copy-start.40
  510.9 7.5 copy-start.46
  510.9 7.5 copy-start.48
  514.6 12.8 %copy-start.9 = (bf16[128,2,4,256]{3,0,2,1:T(8,128)(2,1)}, bf16[128,2,4,256]{3,0,2,1:T(8,128)(2,1)S(1)}, u32[]{:S(2)}) copy-start(bf16[128,2,4,256]{3,0,2,1:T(8,128)(2,1)S(1)} %collective-permute-done.15) | copy-start | bytes 1572868
  514.7 11.3 %collective-permute-start.16 = (bf16[128,4,1,256]{3,0,2,1:T(8,128)(2,1)S(1)}, bf16[128,4,1,256]{3,0,2,1:T(8,128)(2,1)S(1)}, u32[]{:S(2)}, u32[]{:S(2)}) collective-permute-start(bf16[128,4,1,256]{3,0,2,1:T(8,128)(2,1)S(1)} %get-tuple-element.142), channel_id=1, source_target_pairs={{0,2},{2,4},{4,6},{6,8},{8,10},{10,12},{12,14},{14,16},{16,18},{18... | collective-permute-start | bytes 786440 | tf_op jit(solution)/shard_map/ppermute | solution.py:17
  517.0 9.0 %collective-permute-start.17 = (bf16[128,4,1,256]{3,0,2,1:T(8,128)(2,1)S(1)}, bf16[128,4,1,256]{3,0,2,1:T(8,128)(2,1)S(1)}, u32[]{:S(2)}, u32[]{:S(2)}) collective-permute-start(bf16[128,4,1,256]{3,0,2,1:T(8,128)(2,1)S(1)} %get-tuple-element.143), channel_id=1, source_target_pairs={{2,0},{4,2},{6,4},{8,6},{10,8},{12,10},{14,12},{16,14},{18,16},{20... | collective-permute-start | bytes 786440 | tf_op jit(solution)/shard_map/ppermute | solution.py:19
  519.0 7.1 copy-start.74
  520.7 18.5 %collective-permute-start.11 = (bf16[128,4,1,256]{3,0,2,1:T(8,128)(2,1)}, bf16[128,4,1,256]{3,0,2,1:T(8,128)(2,1)S(1)}, u32[]{:S(2)}, u32[]{:S(2)}) collective-permute-start(bf16[128,4,1,256]{3,0,2,1:T(8,128)(2,1)} %get-tuple-element.146), channel_id=1, source_target_pairs={{0,2},{2,4},{4,6},{6,8},{8,10},{10,12},{12,14},{14,16},{16,18},{18... | collective-permute-start | bytes 786440 | tf_op jit(solution)/shard_map/ppermute | solution.py:17
  524.7 14.5 %collective-permute-start.12 = (bf16[128,4,1,256]{3,0,2,1:T(8,128)(2,1)}, bf16[128,4,1,256]{3,0,2,1:T(8,128)(2,1)S(1)}, u32[]{:S(2)}, u32[]{:S(2)}) collective-permute-start(bf16[128,4,1,256]{3,0,2,1:T(8,128)(2,1)} %get-tuple-element.147), channel_id=1, source_target_pairs={{2,0},{4,2},{6,4},{8,6},{10,8},{12,10},{14,12},{16,14},{18,16},{20... | collective-permute-start | bytes 786440 | tf_op jit(solution)/shard_map/ppermute | solution.py:19
  530.4 18.8 %collective-permute-start.18 = (bf16[128,4,6,1]{0,1,3,2:T(4,128)(2,1)S(1)}, bf16[128,4,6,1]{0,1,3,2:T(4,128)(2,1)S(1)}, u32[]{:S(2)}, u32[]{:S(2)}) collective-permute-start(bf16[128,4,6,1]{0,1,3,2:T(4,128)(2,1)S(1)} %copy.267), channel_id=1, source_target_pairs={{0,1},{2,3},{4,5},{6,7},{8,9},{10,11},{12,13},{14,15},{16,17},{18,... | collective-permute-start | bytes 18440 | tf_op jit(solution)/shard_map/ppermute | solution.py:17
  532.6 6.6 copy-start.7
  532.6 17.1 %collective-permute-start.19 = (bf16[128,4,6,1]{0,1,3,2:T(4,128)(2,1)}, bf16[128,4,6,1]{0,1,3,2:T(4,128)(2,1)}, u32[]{:S(2)}, u32[]{:S(2)}) collective-permute-start(bf16[128,4,6,1]{0,1,3,2:T(4,128)(2,1)} %copy.269), channel_id=1, source_target_pairs={{1,0},{3,2},{5,4},{7,6},{9,8},{11,10},{13,12},{15,14},{17,16},{19,... | collective-permute-start | bytes 18440 | tf_op jit(solution)/shard_map/ppermute | solution.py:19
  543.8 18.3 %collective-permute-start.13 = (bf16[128,4,6,1]{0,1,3,2:T(4,128)(2,1)S(1)}, bf16[128,4,6,1]{0,1,3,2:T(4,128)(2,1)S(1)}, u32[]{:S(2)}, u32[]{:S(2)}) collective-permute-start(bf16[128,4,6,1]{0,1,3,2:T(4,128)(2,1)S(1)} %copy.244), channel_id=1, source_target_pairs={{1,0},{3,2},{5,4},{7,6},{9,8},{11,10},{13,12},{15,14},{17,16},{19,... | collective-permute-start | bytes 18440 | tf_op jit(solution)/shard_map/ppermute | solution.py:19
  546.5 16.0 %collective-permute-start.14 = (bf16[128,4,6,1]{0,1,3,2:T(4,128)(2,1)S(1)}, bf16[128,4,6,1]{0,1,3,2:T(4,128)(2,1)S(1)}, u32[]{:S(2)}, u32[]{:S(2)}) collective-permute-start(bf16[128,4,6,1]{0,1,3,2:T(4,128)(2,1)S(1)} %copy.246), channel_id=1, source_target_pairs={{0,1},{2,3},{4,5},{6,7},{8,9},{10,11},{12,13},{14,15},{16,17},{18,... | collective-permute-start | bytes 18440 | tf_op jit(solution)/shard_map/ppermute | solution.py:17
  548.0 3.6 copy-start.5
  548.0 3.6 copy-start.10
  549.2 2.4 copy-start.32
  549.3 2.4 copy-start.34
  571.5 2.0 copy-start.72
  596.7 2.7 copy-start.68
  602.2 2.2 copy-start.69
  604.4 2.7 copy-start.88
  604.5 2.7 copy-start.91
  617.8 2.0 copy-start.15
  634.6 73.7 %copy-start.70 = (bf16[128,2,4,256]{3,2,1,0:T(4,128)(2,1)S(1)}, bf16[128,2,4,256]{3,2,1,0:T(4,128)(2,1)}, u32[]{:S(2)}) copy-start(bf16[128,2,4,256]{3,2,1,0:T(4,128)(2,1)} %param.11) | copy-start | bytes 1572868
  774.7 2.8 copy-start.73
  (87 other events, 110.1 us)
Sparse Core Ops, SparseCore 0:
  617.9 156.6 all-reduce.4
where the time goes:
time: 796 us; the launch traced here: 786 us
  blocking collectives  402 us (51%)
  local copies, waits for them, and re-layouts  147 us (18%)
  waiting for transfers between devices  67.4 us (8%)
  other arithmetic  63.5 us (8%)
  starting transfers between devices  47.1 us (6%)
  matrix products  42.9 us (5%)
  between operations  16.4 us (2%)
    psum x6, blocking collectives, across(): return lax.psum(terms, ('tm', 'height', 'width'))  402 us
    psum x1, waiting for transfers between devices, reduce_weights(): result = lax.psum(terms, ('tm', 'height', 'width'))  64.3 us
    unnamed x283, local copies, waits for them, and re-layouts  37.5 us
    concatenate x18, local copies, waits for them, and re-layouts, tap_stack(): jnp.concatenate(pieces, axis=0).reshape(len(col_taps) * padded.shape[0], -1)  36.9 us
    concatenate x21, other arithmetic, tap_stack(): jnp.concatenate(pieces, axis=0).reshape(len(col_taps) * padded.shape[0], -1)  28.1 us
    slice x12, local copies, waits for them, and re-layouts, tap_stack(): padded[:, first:first + frame_count, top:top + row_count, col_tap:col_tap...  27.9 us
    concatenate x11, other arithmetic, padded_2(): jnp.concatenate([lax.ppermute(tail, axis, [(i, (i + 1) % count) for i in...  21 us
    ppermute x8, starting transfers between devices, padded_2(): lax.ppermute(head, axis, [((i + 1) % count, i) for i in range(ends)])  19 us
  transfers between devices with their start and end apart: 21, of which 2 were waited for; matrix products, arithmetic and copies ran while one was open for 19% of the time, Pallas kernels for 0%

commit v1 on v0

v1 whole, which is shorter than its diff:
```python
import functools

import jax
import jax.numpy as jnp
from jax import lax
from jax.experimental import pallas as pl
from jax.experimental.pallas import tpu as pltpu
from jax.sharding import PartitionSpec as P

MESH = pl.DeviceIdType.MESH
EPS = 1e-05
CH = 128
F32 = jnp.float32
BF16 = jnp.bfloat16


def group_sum(row):
    lane = lax.broadcasted_iota(jnp.int32, row.shape, 1)
    pair = row + jnp.where(lane % 2 == 0, pltpu.roll(row, CH - 1, 1), pltpu.roll(row, 1, 1))
    return pair + jnp.where(lane % 4 < 2, pltpu.roll(pair, CH - 2, 1), pltpu.roll(pair, 2, 1))


def fold_rows(cells):
    return jnp.sum(cells.reshape(-1, 8, CH), axis=0)


def total_row(partial):
    return jnp.sum(partial, axis=0, keepdims=True)


def tile_of(first, second):
    place = lax.broadcasted_iota(jnp.int32, (8, CH), 0)
    return jnp.where(place == 0, first, jnp.where(place == 1, second, 0.0))


def sigmoid(value):
    return 1.0 / (1.0 + jnp.exp(-value))


def body(
    sizes,
    xl, cl, w1, w2, scale_ref, gain1_ref, shift1_ref, gain2_ref, shift2_ref,
    out_ref, o1_ref, o2_ref,
    xr, cr, xe, ce, xeb, ceb, xex, cex, s1, sc, sh, hid, g2, g1, nrm, act_t, hg_t, hg, eh, heb,
    wf1, wb1, wb2, pre1, s_out, s_in, rb1, rb2, a, r0, b1, r1, b2, r2, r3, g3,
    in_send, in_recv, in_local, red_send, red_recv, halo_send, halo_recv, back_send, back_recv, back_local,
    ar_send, ar_recv,
):
    nz, nh, nx, ny = sizes
    ns = nx
    fl, rl, cols = xl.shape[0], xl.shape[1], xl.shape[2]
    strip = cols // nz
    frames = fl * nz
    cells = rl * strip
    z, h, w = lax.axis_index("tm"), lax.axis_index("height"), lax.axis_index("width")
    hx, hy = h // ny, h % ny

    def dev(dz, dh, dw):
        return (lax.rem(z + dz + nz, nz), lax.rem(h + dh + nh, nh), lax.rem(w + dw, 2))

    barrier = pltpu.get_barrier_semaphore()
    partners = [(dz, dh, dw) for dz in range(nz) for dh in (-1, 0, 1) for dw in range(2) if (dz, dh, dw) != (0, 0, 0)]
    partners += [(0, dh, 0) for dh in range(2, nh - 1)]
    for offset in partners:
        pl.semaphore_signal(barrier, inc=1, device_id=dev(*offset), device_id_type=MESH)
    pl.semaphore_wait(barrier, len(partners))

    def remote(src, dst, send, recv, where):
        return pltpu.make_async_remote_copy(
            src_ref=src, dst_ref=dst, send_sem=send, recv_sem=recv, device_id=where, device_id_type=MESH
        )

    own_frames = pl.ds(z * fl, fl)
    row_parts = {0: ((0, rl), (1, rl)), 1: ((rl - 1, 1), (0, 1)), -1: ((0, 1), (rl + 1, 1))}

    def main_copies(k, src, dst):
        copies = []
        for dz in range(nz):
            q = lax.rem(z + dz, nz)
            for n, dh in enumerate((0, 1, -1)):
                (r_from, count), (r_to, _) = row_parts[dh]
                source = src.at[:, pl.ds(r_from, count), pl.ds(pl.multiple_of(q * strip, strip), strip), :]
                target = dst.at[own_frames, pl.ds(r_to, count)]
                if dz == 0 and dh == 0:
                    copies.append(pltpu.make_async_copy(source, target, in_local.at[k, 0]))
                else:
                    place = dz * 3 + n
                    copies.append(
                        remote(source, target, in_send.at[k, place], in_recv.at[k, place], dev(dz, dh, 0))
                    )
        return copies

    def build_edges(src, edges):
        def at(f, r, col):
            start = (col // 16) * 16
            return src[f, r, start : start + 16, :].astype(F32)[col % 16 : col % 16 + 1]

        place = lax.broadcasted_iota(jnp.int32, (16, CH), 0)
        for f in range(fl):
            for q in range(nz):
                tile = jnp.zeros((16, CH), F32)
                for r in range(rl):
                    if q > 0:
                        tile = jnp.where(place == 2 * r, at(f, r, q * strip - 1), tile)
                    if q < nz - 1:
                        tile = jnp.where(place == 2 * r + 1, at(f, r, (q + 1) * strip), tile)
                edges[q, f] = tile.astype(BF16)
            tile = jnp.zeros((16, CH), F32)
            for r in range(rl):
                outer = jnp.where(w == 0, at(f, r, cols - 1), at(f, r, 0))
                tile = jnp.where(place // 2 == r, outer, tile)
            edges[nz, f] = tile.astype(BF16)

    def edge_copies(k, edges, landing, landing_out):
        copies = []
        base = 3 * nz
        for dz in range(nz):
            q = lax.rem(z + dz, nz)
            for n, dh in enumerate((0, 1, -1)):
                source = edges.at[q]
                target = landing.at[1 - dh, own_frames]
                place = base + dz * 3 + n
                if dz == 0 and dh == 0:
                    copies.append(pltpu.make_async_copy(source, target, in_local.at[k, 1]))
                else:
                    copies.append(
                        remote(source, target, in_send.at[k, place], in_recv.at[k, place], dev(dz, dh, 0))
                    )
        return copies

    outer_q = (nz - 1) * w
    takes_outer = z == (nz - 1) * (1 - w)

    def outer_sends(k, edges, landing_out):
        copies = []
        base = 6 * nz
        for n, dh in enumerate((0, 1, -1)):
            where = (outer_q, lax.rem(h + dh + nh, nh), 1 - w)
            copies.append(
                remote(
                    edges.at[nz], landing_out.at[1 - dh, own_frames],
                    in_send.at[k, base + n], in_recv.at[k, base + 3 * z + n], where,
                )
            )
        return copies

    def outer_waits(k, edges, landing_out):
        for zs in range(nz):
            for n, dh in enumerate((0, 1, -1)):
                remote(
                    edges.at[nz], landing_out.at[1 - dh, pl.ds(zs * fl, fl)],
                    in_send.at[k, 6 * nz + n], in_recv.at[k, 6 * nz + 3 * zs + n], dev(0, 0, 1),
                ).wait_recv()

    def wait_copies(copies):
        for copy in copies:
            copy.wait()

    x_main = main_copies(0, xl, xr)
    for copy in x_main:
        copy.start()
    build_edges(xl, xe)
    x_edge = edge_copies(0, xe, xeb, xex)
    x_outer = outer_sends(0, xe, xex)
    for copy in x_edge + x_outer:
        copy.start()
    c_main = main_copies(1, cl, cr)
    for copy in c_main:
        copy.start()

    me8 = z * 2 + w

    def red1_copies(k):
        copies = []
        for n, (dz, dw) in enumerate([(dz, dw) for dz in range(nz) for dw in range(2) if (dz, dw) != (0, 0)]):
            slot = rb1.at[k, me8]
            copies.append(remote(slot, slot, red_send.at[k, n], red_recv.at[k, n], dev(dz, 0, dw)))
        return copies

    def red2_copies(k):
        copies = []
        for dh in range(1, nh):
            slot = rb2.at[k, h]
            n = 2 * nz + dh
            copies.append(remote(slot, slot, red_send.at[k, n], red_recv.at[k, n], dev(0, dh, 0)))
        return copies

    def start_all(copies):
        for copy in copies:
            copy.start()

    def red1_start(k, tile):
        rb1[k, me8] = tile
        start_all(red1_copies(k))

    def red2_start(k, tile):
        rb2[k, h] = tile
        start_all(red2_copies(k))

    def moments(buffer, k, count, size):
        mean = jnp.sum(buffer[k, :, 0:1, :], axis=0) / count
        spread = jnp.zeros((1, CH), F32)
        for n in range(count):
            off = buffer[k, n, 0:1, :] - mean
            spread = spread + (buffer[k, n, 1:2, :] + size * off * off)
        return mean, spread

    def plain_sums(buffer, k):
        return jnp.sum(buffer[k], axis=0)

    local_size = 4.0 * fl * rl * cols
    total_size = local_size * 2 * nz * nh

    def moments_mid(k):
        wait_copies(red1_copies(k))
        mean, spread = moments(rb1, k, 2 * nz, local_size)
        red2_start(k, tile_of(mean, spread))

    def moments_end(k):
        wait_copies(red2_copies(k))
        return moments(rb2, k, nh, local_size * 2 * nz)

    def sums_mid(k):
        wait_copies(red1_copies(k))
        red2_start(k, plain_sums(rb1, k))

    def sums_end(k):
        wait_copies(red2_copies(k))
        sums = plain_sums(rb2, k) / total_size
        return sums[0:1], sums[1:2]

    zero8 = jnp.zeros((8, CH), F32)

    def x_sum(n, total):
        return total + fold_rows(xl[n // rl, n % rl].astype(F32))

    local_mean = group_sum(total_row(lax.fori_loop(0, fl * rl, x_sum, zero8))) / local_size

    def x_spread(n, total):
        off = xl[n // rl, n % rl].astype(F32) - local_mean
        return total + fold_rows(off * off)

    local_spread = group_sum(total_row(lax.fori_loop(0, fl * rl, x_spread, zero8)))
    red1_start(0, tile_of(local_mean, local_spread))

    build_edges(cl, ce)
    c_edge = edge_copies(1, ce, ceb, cex)
    c_outer = outer_sends(1, ce, cex)
    start_all(c_edge + c_outer)

    for kt in range(3):
        for kr in range(3):
            for kc in range(3):
                tap = 9 * kt + 3 * kr + kc
                back = ((2 - kr) * 3 + (2 - kc)) * CH
                for source, target in ((w1, wb1), (w2, wb2)):
                    target[back : back + CH, kt * CH : (kt + 1) * CH] = source[:, tap * CH : (tap + 1) * CH]
    moments_mid(0)
    for kt in range(3):
        for kr in range(3):
            for kc in range(3):
                tap = 9 * kt + 3 * kr + kc
                ahead = (kr * 3 + kc) * CH
                block = w1[:, tap * CH : (tap + 1) * CH].astype(F32)
                wf1[ahead : ahead + CH, (2 - kt) * CH : (3 - kt) * CH] = jnp.transpose(block).astype(BF16)
    zero_cells = jnp.zeros((cells, CH), F32)

    def clear(n, _):
        hid[n] = zero_cells
        g2[n] = zero_cells
        g1[n] = zero_cells
        return 0

    lax.fori_loop(0, frames + 2, clear, 0)
    zero_t = jnp.zeros((2 * CH, cells), BF16)
    act_t[0 : 2 * CH] = zero_t
    hg_t[frames * CH : (frames + 2) * CH] = zero_t

    row_place = lax.broadcasted_iota(jnp.int32, (strip, CH), 0)
    left_ok = jnp.logical_not(jnp.logical_and(w == 0, z == 0))
    right_ok = jnp.logical_not(jnp.logical_and(w == 1, z == nz - 1))

    def row_ok(r):
        if r == 0:
            return h > 0
        if r == rl + 1:
            return h < nh - 1
        return None

    def row_source(r):
        if r == 0:
            return 0, rl - 1
        if r == rl + 1:
            return 2, 0
        return 1, r - 1

    def store_stack(stack, f, r, value, left, right):
        ok = row_ok(r)
        left = jnp.where(left_ok if ok is None else jnp.logical_and(left_ok, ok), left, 0.0)
        right = jnp.where(right_ok if ok is None else jnp.logical_and(right_ok, ok), right, 0.0)
        if ok is not None:
            value = jnp.where(ok, value, 0.0)
        before = jnp.where(row_place == 0, left, pltpu.roll(value, 1, 0))
        after = jnp.where(row_place == strip - 1, right, pltpu.roll(value, strip - 1, 0))
        stack[f, r, :, 0:CH] = before.astype(BF16)
        stack[f, r, :, CH : 2 * CH] = value.astype(BF16)
        stack[f, r, :, 2 * CH : 3 * CH] = after.astype(BF16)

    edge_place = lax.broadcasted_iota(jnp.int32, (16, CH), 0)
    outer_mask = jnp.logical_and(takes_outer, edge_place % 2 == 1 - w)

    def input_stack(stack, source, landing, landing_out, apply):
        def step(f, _):
            edges = []
            for d in range(3):
                tile = jnp.where(outer_mask, landing_out[d, f].astype(F32), landing[d, f].astype(F32))
                edges.append(apply(tile))
            for r in range(rl + 2):
                d, row = row_source(r)
                tile = edges[d]
                store_stack(
                    stack, f, r, apply(source[f, r].astype(F32)),
                    tile[2 * row : 2 * row + 1], tile[2 * row + 1 : 2 * row + 2],
                )
            return 0

        lax.fori_loop(0, frames, step, 0)

    def window(stack, f):
        return [stack[f, kr : kr + rl].reshape(cells, 3 * CH) for kr in range(3)]

    def convolve(stack, weight, target):
        def step(f, _):
            product = jnp.dot(
                jnp.concatenate(window(stack, f), axis=1), weight[...], preferred_element_type=F32
            )
            for j in range(3):
                target[f + j] += product[:, j * CH : (j + 1) * CH]
            return 0

        lax.fori_loop(0, frames, step, 0)

    def weight_part(turned, stack, kr):
        left = jnp.concatenate([turned[f * CH : (f + 3) * CH, :] for f in range(frames)], axis=1)
        right = stack[:, kr : kr + rl].reshape(frames * cells, 3 * CH)
        return jnp.dot(left, right, preferred_element_type=F32)

    def peer(axis, j):
        if axis == "z":
            return dev(j, 0, 0)
        if axis == "x":
            return (z, lax.rem(hx + j, nx) * ny + hy, w)
        return (z, hx * ny + lax.rem(hy + j, ny), w)

    coords = {"z": z, "x": hx, "y": hy}
    orders = (("z", "y", "x"), ("y", "x", "z"), ("x", "z", "y"))
    half = 8
    span = half // ns
    tiles = span * 9
    piece = -(-tiles // ns)
    outs = (o1_ref, o2_ref)
    step_at = {"core": 0, "a1": 1, "a2": 1 + (ns - 1), "a3": 1 + 2 * (ns - 1), "g2": 1 + 3 * (ns - 1),
               "g1": 1 + 4 * (ns - 1), "gc": 1 + 5 * (ns - 1)}

    def sems(g, p, stage, n):
        return ar_send.at[g, p, step_at[stage] + n], ar_recv.at[g, p, step_at[stage] + n]

    def core_copy(g, p):
        return remote(a.at[g, p, pl.ds((1 - w) * half, half)], r0.at[g, p], *sems(g, p, "core", 0), dev(0, 0, 1))

    def core_start(g, p):
        core_copy(g, p).start()

    def a1_copies(g, p):
        axis = orders[p][0]
        return [
            remote(
                b1.at[g, p, pl.ds(lax.rem(coords[axis] + j, ns) * span, span)], r1.at[g, p, j - 1],
                *sems(g, p, "a1", j - 1), peer(axis, j),
            )
            for j in range(1, ns)
        ]

    def a1_start(g, p):
        core_copy(g, p).wait()
        b1[g, p] = a[g, p, pl.ds(w * half, half)] + r0[g, p]
        start_all(a1_copies(g, p))

    def a2_copies(g, p):
        axis = orders[p][1]
        return [
            remote(
                b2.at[g, p, pl.ds(lax.rem(coords[axis] + j, ns) * piece, piece)], r2.at[g, p, j - 1],
                *sems(g, p, "a2", j - 1), peer(axis, j),
            )
            for j in range(1, ns)
        ]

    def a2_start(g, p):
        wait_copies(a1_copies(g, p))
        value = b1[g, p, pl.ds(coords[orders[p][0]] * span, span)]
        for j in range(ns - 1):
            value = value + r1[g, p, j]
        b2[g, p, 0:tiles] = value.reshape(tiles, 8, CH)
        if piece * ns > tiles:
            b2[g, p, tiles:] = jnp.zeros((piece * ns - tiles, 8, CH), F32)
        start_all(a2_copies(g, p))

    def a3_copies(g, p):
        axis = orders[p][2]
        slot = r3.at[g, p, coords[axis]]
        return [remote(slot, slot, *sems(g, p, "a3", j - 1), peer(axis, j)) for j in range(1, ns)]

    def a3_start(g, p):
        wait_copies(a2_copies(g, p))
        value = b2[g, p, pl.ds(coords[orders[p][1]] * piece, piece)]
        for j in range(ns - 1):
            value = value + r2[g, p, j]
        r3[g, p, coords[orders[p][2]]] = value
        start_all(a3_copies(g, p))

    def g2_copies(g, p):
        axis = orders[p][1]
        part = g3.at[g, p, pl.ds(coords[axis] * piece, piece)]
        return [remote(part, part, *sems(g, p, "g2", j - 1), peer(axis, j)) for j in range(1, ns)]

    def g2_start(g, p):
        wait_copies(a3_copies(g, p))
        value = r3[g, p, 0]
        for n in range(1, ns):
            value = value + r3[g, p, n]
        g3[g, p, pl.ds(coords[orders[p][1]] * piece, piece)] = value
        start_all(g2_copies(g, p))

    def out_span(g, p, n):
        return outs[g].at[p, pl.ds(w * half + n * span, span)]

    def g1_copies(g, p):
        axis = orders[p][0]
        part = out_span(g, p, coords[axis])
        return [remote(part, part, *sems(g, p, "g1", j - 1), peer(axis, j)) for j in range(1, ns)]

    def gc_copy(g, p, j):
        part = out_span(g, p, lax.rem(coords[orders[p][0]] + ns - j, ns))
        return remote(part, part, *sems(g, p, "gc", j), dev(0, 0, 1))

    def g1_start(g, p):
        wait_copies(g2_copies(g, p))
        outs[g][p, pl.ds(w * half + coords[orders[p][0]] * span, span)] = g3[g, p, 0:tiles].reshape(span, 9, 8, CH)
        start_all(g1_copies(g, p))
        gc_copy(g, p, 0).start()

    def gc_start(g, p):
        for j, copy in enumerate(g1_copies(g, p)):
            copy.wait()
            gc_copy(g, p, j + 1).start()

    def gc_end(g, p):
        for j in range(ns):
            gc_copy(g, p, j).wait()

    def each(stage, g):
        for p in range(3):
            stage(g, p)

    mean1, spread1 = moments_end(0)
    scale = scale_ref[...]
    inv1 = 1.0 / jnp.sqrt(spread1 * (scale * scale) / total_size + EPS)
    factor1 = scale * inv1
    gain1, shift1 = gain1_ref[...], shift1_ref[...]
    gain2, shift2 = gain2_ref[...], shift2_ref[...]

    def rounded(value):
        return value.astype(BF16).astype(F32)

    def act_first(value):
        pre = (value - mean1) * factor1 * gain1 + shift1
        return rounded(pre * sigmoid(pre))

    wait_copies(x_main + x_edge)
    for copy in x_outer:
        copy.wait_send()

    @pl.when(takes_outer)
    def _():
        outer_waits(0, xe, xex)

    input_stack(s1, xr, xeb, xex, act_first)
    convolve(s1, wf1, hid)

    def hid_sum(n, total):
        return total + fold_rows(hid[n])

    mean_l = group_sum(total_row(lax.fori_loop(0, frames, hid_sum, zero8))) / local_size

    def hid_spread(n, total):
        off = hid[n] - mean_l
        return total + fold_rows(off * off)

    red1_start(1, tile_of(mean_l, group_sum(total_row(lax.fori_loop(0, frames, hid_spread, zero8)))))

    wait_copies(c_main + c_edge)
    for copy in c_outer:
        copy.wait_send()

    @pl.when(takes_outer)
    def _():
        outer_waits(1, ce, cex)

    input_stack(sc, cr, ceb, cex, lambda value: value)
    moments_mid(1)
    convolve(sc, wb2, g2)
    mean2, spread2 = moments_end(1)
    inv2 = 1.0 / jnp.sqrt(spread2 / total_size + EPS)

    def second(n, totals):
        first_total, second_total = totals
        normed = (hid[n] - mean2) * inv2
        pre = normed * gain2 + shift2
        sig = sigmoid(pre)
        act_t[pl.ds(pl.multiple_of((n + 2) * CH, CH), CH), :] = jnp.transpose(pre * sig).astype(BF16)
        scaled = g2[n + 2] * (sig * (1.0 + pre * (1.0 - sig))) * gain2
        nrm[n] = normed
        g2[n + 2] = scaled
        return first_total + fold_rows(scaled), second_total + fold_rows(scaled * normed)

    t1, t2 = lax.fori_loop(0, frames, second, (zero8, zero8))
    red1_start(2, tile_of(group_sum(total_row(t1)), group_sum(total_row(t2))))

    def put_second(kr):
        block = weight_part(act_t, sc, kr)
        for kt in range(3):
            for kc in range(3):
                part = block[kt * CH : (kt + 1) * CH, kc * CH : (kc + 1) * CH]
                a[1, 2 - kr, :, kt * 3 + (2 - kc)] = part.reshape(16, 8, CH)
        core_start(1, 2 - kr)

    put_second(0)
    sums_mid(2)
    put_second(1)
    put_second(2)
    m1, m2 = sums_end(2)

    def hidden(n, _):
        value = inv2 * (g2[n + 2] - m1 - nrm[n] * m2)
        hg_t[pl.ds(pl.multiple_of(n * CH, CH), CH), :] = jnp.transpose(value).astype(BF16)
        narrow = value.astype(BF16)
        hg[n, 1 : rl + 1] = narrow.reshape(rl, strip, CH)
        wide = narrow.astype(F32).reshape(rl, strip, CH)
        lefts = jnp.zeros((16, CH), F32)
        rights = jnp.zeros((16, CH), F32)
        for r in range(rl):
            lefts = jnp.where(edge_place == r, wide[r, 0:1], lefts)
            rights = jnp.where(edge_place == r, wide[r, strip - 1 : strip], rights)
        eh[0, n] = lefts.astype(BF16)
        eh[1, n] = rights.astype(BF16)
        return 0

    lax.fori_loop(0, frames, hidden, 0)

    line = w * nz + z

    def beside(ds, dh):
        place = lax.rem(line + ds + 2 * nz, 2 * nz)
        return (lax.rem(place, nz), lax.rem(h + dh + nh, nh), place // nz)

    halo = [
        remote(hg.at[:, pl.ds(rl, 1)], hg.at[:, pl.ds(0, 1)], halo_send.at[0], halo_recv.at[0], dev(0, 1, 0)),
        remote(hg.at[:, pl.ds(1, 1)], hg.at[:, pl.ds(rl + 1, 1)], halo_send.at[1], halo_recv.at[1], dev(0, -1, 0)),
    ]
    for n, dh in enumerate((0, 1, -1)):
        halo.append(remote(eh.at[0], heb.at[1 - dh, 1], halo_send.at[2 + n], halo_recv.at[2 + n], beside(-1, dh)))
        halo.append(remote(eh.at[1], heb.at[1 - dh, 0], halo_send.at[5 + n], halo_recv.at[5 + n], beside(1, dh)))
    start_all(halo)
    each(a1_start, 1)

    def put_first(kr):
        block = weight_part(hg_t, s1, kr)
        for j in range(3):
            for kc in range(3):
                part = block[j * CH : (j + 1) * CH, kc * CH : (kc + 1) * CH]
                a[0, kr, :, (2 - j) * 3 + kc] = part.reshape(16, 8, CH)
        core_start(0, kr)

    for kr in range(3):
        put_first(kr)
    wait_copies(halo)

    def halo_stack(f, _):
        lefts = [heb[d, 0, f].astype(F32) for d in range(3)]
        rights = [heb[d, 1, f].astype(F32) for d in range(3)]
        for r in range(rl + 2):
            d, row = row_source(r)
            store_stack(sh, f, r, hg[f, r].astype(F32), lefts[d][row : row + 1], rights[d][row : row + 1])
        return 0

    lax.fori_loop(0, frames, halo_stack, 0)
    each(a2_start, 1)
    each(a1_start, 0)
    convolve(sh, wb1, g1)
    each(a3_start, 1)
    each(a2_start, 0)

    def first(f, totals):
        first_total, second_total = totals
        for r in range(rl):
            normed = (xr[f, r + 1].astype(F32) - mean1) * factor1
            pre = normed * gain1 + shift1
            sig = sigmoid(pre)
            scaled = g1[f + 2, r * strip : (r + 1) * strip] * (sig * (1.0 + pre * (1.0 - sig))) * gain1
            s_out[f, r] = scaled.astype(BF16)
            first_total = first_total + fold_rows(scaled)
            second_total = second_total + fold_rows(scaled * normed)
        return first_total, second_total

    t1, t2 = lax.fori_loop(0, frames, first, (zero8, zero8))
    red1_start(3, tile_of(group_sum(total_row(t1)), group_sum(total_row(t2))))

    back_copies = []
    for dz in range(nz):
        q = lax.rem(z + dz, nz)
        source = s_out.at[pl.ds(q * fl, fl)]
        target = s_in.at[:, :, pl.ds(pl.multiple_of(z * strip, strip), strip), :]
        if dz == 0:
            back_copies.append(pltpu.make_async_copy(source, target, back_local.at[0]))
        else:
            back_copies.append(remote(source, target, back_send.at[dz], back_recv.at[dz], dev(dz, 0, 0)))
    start_all(back_copies)
    each(g2_start, 1)
    each(a3_start, 0)
    sums_mid(3)
    each(g1_start, 1)
    each(g2_start, 0)
    m1, m2 = sums_end(3)
    wait_copies(back_copies)
    each(g1_start, 0)

    def last(n, _):
        f, r = n // rl, n % rl
        normed = (xl[f, r].astype(F32) - mean1) * factor1
        out_ref[f, r] = cl[f, r].astype(F32) + inv1 * (s_in[f, r].astype(F32) - m1 - normed * m2)
        return 0

    lax.fori_loop(0, fl * rl, last, 0)
    each(gc_start, 1)
    each(gc_start, 0)
    each(gc_end, 1)
    each(gc_end, 0)


def shards(sizes, latent, exponents, cotangent, conv_first, conv_second, gain_first, shift_first, gain_second, shift_second):
    nz, nh, nx, ny = sizes
    channels, fl, rl, cols = latent.shape
    strip = cols // nz
    frames = fl * nz
    cells = rl * strip
    ns = nx
    span = 8 // ns
    tiles = span * 9
    piece = -(-tiles // ns)
    scale = jnp.repeat(jnp.exp2(exponents.astype(F32)), channels // exponents.shape[0])[None]
    xl = jnp.transpose(latent, (1, 2, 3, 0))
    cl = jnp.transpose(cotangent, (1, 2, 3, 0))
    vmem = pl.BlockSpec(memory_space=pltpu.VMEM)
    n_ar = 1 + 5 * (ns - 1) + ns
    n_in = 6 * nz + 3 * nz
    wide = (frames, rl + 2, strip, 3 * CH)
    scratch = [
        pltpu.VMEM((frames, rl + 2, strip, CH), BF16),
        pltpu.VMEM((frames, rl + 2, strip, CH), BF16),
        pltpu.VMEM((nz + 1, fl, 16, CH), BF16),
        pltpu.VMEM((nz + 1, fl, 16, CH), BF16),
        pltpu.VMEM((3, frames, 16, CH), BF16),
        pltpu.VMEM((3, frames, 16, CH), BF16),
        pltpu.VMEM((3, frames, 16, CH), BF16),
        pltpu.VMEM((3, frames, 16, CH), BF16),
        pltpu.VMEM(wide, BF16),
        pltpu.VMEM(wide, BF16),
        pltpu.VMEM(wide, BF16),
        pltpu.VMEM((frames + 2, cells, CH), F32),
        pltpu.VMEM((frames + 2, cells, CH), F32),
        pltpu.VMEM((frames + 2, cells, CH), F32),
        pltpu.VMEM((frames, cells, CH), F32),
        pltpu.VMEM(((frames + 2) * CH, cells), BF16),
        pltpu.VMEM(((frames + 2) * CH, cells), BF16),
        pltpu.VMEM((frames, rl + 2, strip, CH), BF16),
        pltpu.VMEM((2, frames, 16, CH), BF16),
        pltpu.VMEM((3, 2, frames, 16, CH), BF16),
        pltpu.VMEM((9 * CH, 3 * CH), BF16),
        pltpu.VMEM((9 * CH, 3 * CH), BF16),
        pltpu.VMEM((9 * CH, 3 * CH), BF16),
        pltpu.VMEM((8, CH), F32),
        pltpu.VMEM((frames, rl, strip, CH), BF16),
        pltpu.VMEM((fl, rl, cols, CH), BF16),
        pltpu.VMEM((4, 2 * nz, 8, CH), F32),
        pltpu.VMEM((4, nh, 8, CH), F32),
        pltpu.VMEM((2, 3, 16, 9, 8, CH), F32),
        pltpu.VMEM((2, 3, 8, 9, 8, CH), F32),
        pltpu.VMEM((2, 3, 8, 9, 8, CH), F32),
        pltpu.VMEM((2, 3, ns - 1, span, 9, 8, CH), F32),
        pltpu.VMEM((2, 3, piece * ns, 8, CH), F32),
        pltpu.VMEM((2, 3, ns - 1, piece, 8, CH), F32),
        pltpu.VMEM((2, 3, ns, piece, 8, CH), F32),
        pltpu.VMEM((2, 3, piece * ns, 8, CH), F32),
        pltpu.SemaphoreType.DMA((2, n_in)),
        pltpu.SemaphoreType.DMA((2, n_in)),
        pltpu.SemaphoreType.DMA((2, 2)),
        pltpu.SemaphoreType.DMA((4, 2 * nz + nh)),
        pltpu.SemaphoreType.DMA((4, 2 * nz + nh)),
        pltpu.SemaphoreType.DMA((8,)),
        pltpu.SemaphoreType.DMA((8,)),
        pltpu.SemaphoreType.DMA((nz,)),
        pltpu.SemaphoreType.DMA((nz,)),
        pltpu.SemaphoreType.DMA((1,)),
        pltpu.SemaphoreType.DMA((2, 3, n_ar)),
        pltpu.SemaphoreType.DMA((2, 3, n_ar)),
    ]
    grad, first, second = pl.pallas_call(
        functools.partial(body, sizes),
        out_shape=(
            jax.ShapeDtypeStruct((fl, rl, cols, CH), F32),
            jax.ShapeDtypeStruct((3, 16, 9, 8, CH), F32),
            jax.ShapeDtypeStruct((3, 16, 9, 8, CH), F32),
        ),
        in_specs=[vmem] * 9,
        out_specs=(vmem, vmem, vmem),
        scratch_shapes=scratch,
        compiler_params=pltpu.CompilerParams(
            collective_id=0, has_side_effects=True, vmem_limit_bytes=60 * 1024 * 1024
        ),
    )(
        xl, cl, conv_first, conv_second, scale,
        gain_first[None], shift_first[None], gain_second[None], shift_second[None],
    )
    first = first.reshape(3, 16, 3, 3, 8, CH).transpose(1, 4, 2, 0, 3, 5).reshape(CH, 27 * CH)
    second = second.reshape(3, 16, 3, 3, 8, CH).transpose(5, 2, 0, 3, 1, 4).reshape(CH, 27 * CH)
    return jnp.transpose(grad, (3, 0, 1, 2)), first, second


def solution(mesh):
    nz, nh = mesh.shape["tm"], mesh.shape["height"]
    nx = int(round(nh**0.5))
    placed = P(None, "tm", "height", "width")
    return jax.shard_map(
        functools.partial(shards, (nz, nh, nx, nh // nx)),
        mesh=mesh,
        in_specs=(placed, P(), placed, P(), P(), P(), P(), P(), P()),
        out_specs=(placed, P(), P()),
        check_vma=False,
    )
```

time: 796 us -> 124 us (0.16); the launches traced: 786 us -> 124 us
  blocking collectives: 402 us -> 0 us
  local copies, waits for them, and re-layouts: 147 us -> 12.1 us
  Pallas kernels: 0 us -> 110 us
  waiting for transfers between devices: 67.4 us -> 0 us
  other arithmetic: 63.5 us -> 0.66 us
  starting transfers between devices: 47.1 us -> 0 us
  matrix products: 42.9 us -> 0 us
  between operations: 16.4 us -> 0.66 us
    psum x6 -> x0, blocking collectives: 402 us -> none  [across(): return lax.psum(terms, ('tm', 'height', 'width'))]
    pallas_call x0 -> x1, Pallas kernels: none -> 110 us  [shards(): pl.pallas_call(functools.partial(body, sizes), out_shape=(jax.ShapeDtypeS...]
    psum x1 -> x0, waiting for transfers between devices: 64.3 us -> none  [reduce_weights(): result = lax.psum(terms, ('tm', 'height', 'width'))]
    concatenate x32 -> x0, other arithmetic: 49.1 us -> none  [the longest x21 28.1 us: tap_stack(): jnp.concatenate(pieces, axis=0).reshape(len(col_taps) * padded.shape[0], -1)]
    ppermute x20 -> x0, starting transfers between devices: 47.1 us -> none  [the longest x8 19 us: padded_2(): lax.ppermute(head, axis, [((i + 1) % count, i) for i in range(ends)])]
    dot_general x45 -> x0, matrix products: 42.9 us -> none  [the longest x18 18.1 us: weight_terms(): lax.dot_general(flat_grad, stacked, (((1,), (1,)), ((), ())), preferred_e...]
    slice x26 -> x0, local copies, waits for them, and re-layouts: 41.4 us -> none  [the longest x12 27.9 us: tap_stack(): padded[:, first:first + frame_count, top:top + row_count, col_tap:col_tap...]
    concatenate x18 -> x0, local copies, waits for them, and re-layouts: 36.9 us -> none  [tap_stack(): jnp.concatenate(pieces, axis=0).reshape(len(col_taps) * padded.shape[0], -1)]
  transfers between devices with their start and end apart: 21 -> 0, of which waited for: 2 -> 0; matrix products, arithmetic and copies ran while one was open for 19% -> 0% of each run, Pallas kernels for 0% -> 0%
where the time goes in v1:
time: 124 us
  Pallas kernels  110 us (89%)
  local copies, waits for them, and re-layouts  12.1 us (10%)
    pallas_call x1, Pallas kernels, shards(): pl.pallas_call(functools.partial(body, sizes), out_shape=(jax.ShapeDtypeS...  110 us
    unnamed x8, local copies, waits for them, and re-layouts  9.9 us

profile of v1, /device:TPU:1, one launch (start us, length us, event | category | flops | bytes accessed | tf_op | source)
XLA Modules:
  0.0 123.5 jit_solution(5265693983284674459)
XLA Ops:
  0.6 0.7 multiply_exponential_fusion
  1.3 0.1 broadcast_in_dim.15
  1.4 0.6 broadcast_in_dim_reshape.3.scale_ref
  2.0 2.2 %copy.17 = bf16[128,2,4,256]{0,3,2,1:T(8,128)(2,1)} copy(bf16[128,2,4,256]{3,2,1,0:T(4,128)(2,1)} %param.9) | data formatting | bytes 1048576 | tf_op args[0]
  4.2 2.2 %copy.18 = bf16[128,2,4,256]{0,3,2,1:T(8,128)(2,1)} copy(bf16[128,2,4,256]{3,2,1,0:T(4,128)(2,1)} %param.11) | data formatting | bytes 1048576 | tf_op args[2]
  6.4 110.1 %shard_map.112 = (f32[2,4,256,128]{3,2,1,0:T(8,128)}, f32[3,16,9,8,128]{4,3,2,1,0:T(8,128)}, f32[3,16,9,8,128]{4,3,2,1,0:T(8,128)}) custom-call(bf16[2,4,256,128]{3,2,1,0:T(8,128)(2,1)} %bitcast.16, bf16[2,4,256,128]{3,2,1,0:T(8,128)(2,1)} %bitcast.17, bf16[128,3456]{1,0:T(8,128)(2,1)} %w1.1, bf16[128,3456]{1,0:T(8,128)(2,1)} %w2.1, ...), custom_call_target="tpu_custom_call" | custom-call | tf_op jit(solution)/shard_map/pallas_call | solution.py:718
  116.5 0.0 copy-start.1
  116.5 2.7 %copy.21 = f32[128,2,4,256]{3,2,1,0:T(4,128)} copy(f32[128,2,4,256]{0,3,2,1:T(8,128)} %bitcast.21) | data formatting | bytes 2097152
  119.3 0.0 copy-done.1
  119.3 0.0 copy-start
  119.3 1.3 %copy.19 = f32[16,8,3,3,3,128]{5,1,4,3,2,0:T(8,128)} copy(f32[16,8,3,3,3,128]{5,1,4,2,0,3:T(8,128)S(1)} %bitcast.20) | data formatting | bytes 3538944 | tf_op jit(solution)/shard_map/transpose | solution.py:735
  120.6 0.8 copy-done
  121.4 0.2 copy.20
  121.6 1.9 %copy.22 = f32[128,3456]{1,0:T(8,128)} copy(f32[128,3456]{0,1:T(8,128)S(1)} %bitcast.15) | data formatting | bytes 3538944
Async XLA Ops:
  116.5 2.7 %copy-start.1 = (f32[3,16,9,8,128]{4,3,2,1,0:T(8,128)S(1)}, f32[3,16,9,8,128]{4,3,2,1,0:T(8,128)}, u32[]{:S(2)}) copy-start(f32[3,16,9,8,128]{4,3,2,1,0:T(8,128)} %get-tuple-element.7) | copy-start | bytes 5308420
  119.3 2.1 %copy-start = (f32[3,16,9,8,128]{4,3,2,1,0:T(8,128)S(1)}, f32[3,16,9,8,128]{4,3,2,1,0:T(8,128)}, u32[]{:S(2)}) copy-start(f32[3,16,9,8,128]{4,3,2,1,0:T(8,128)} %get-tuple-element.8) | copy-start | bytes 5308420

commit v2 on v1

--- a/solution.py
+++ b/solution.py
@@ -28,9 +28,23 @@
     return jnp.sum(partial, axis=0, keepdims=True)
 
 
-def tile_of(first, second):
-    place = lax.broadcasted_iota(jnp.int32, (8, CH), 0)
-    return jnp.where(place == 0, first, jnp.where(place == 1, second, 0.0))
+def lanes_low(row):
+    return lax.broadcasted_iota(jnp.int32, row.shape, row.ndim - 1) % 4 < 2
+
+
+def pack_pair(first, second):
+    return jnp.where(lanes_low(first), first, second)
+
+
+def unpack_pair(row):
+    low = lanes_low(row)
+    return jnp.where(low, row, pltpu.roll(row, 2, 1)), jnp.where(low, pltpu.roll(row, CH - 2, 1), row)
+
+
+def far_first(n, size):
+    if size == 4:
+        return (2 + 3 * n + 3 * ((n * (n - 1)) // 2)) % 4
+    return size - 1 - n
 
 
 def sigmoid(value):
@@ -39,11 +53,12 @@
 
 def body(
     sizes,
-    xl, cl, w1, w2, scale_ref, gain1_ref, shift1_ref, gain2_ref, shift2_ref,
-    out_ref, o1_ref, o2_ref,
+    xl, cl_hbm, w1_hbm, w2_hbm, exponent_ref, gain1_ref, shift1_ref, gain2_ref, shift2_ref,
+    out_hbm, o1_hbm, o2_hbm,
+    cl, w1, w2, out_ref, o1_ref, o2_ref,
     xr, cr, xe, ce, xeb, ceb, xex, cex, s1, sc, sh, hid, g2, g1, nrm, act_t, hg_t, hg, eh, heb,
-    wf1, wb1, wb2, pre1, s_out, s_in, rb1, rb2, a, r0, b1, r1, b2, r2, r3, g3,
-    in_send, in_recv, in_local, red_send, red_recv, halo_send, halo_recv, back_send, back_recv, back_local,
+    wf1, wb1, wb2, s_out, s_in, rb, a, r0, b1, r1, b2, r2, r3, g3,
+    load_sem, store_sem, in_send, in_recv, red_send, red_recv, halo_send, halo_recv, back_send, back_recv,
     ar_send, ar_recv,
 ):
     nz, nh, nx, ny = sizes
@@ -58,12 +73,41 @@
     def dev(dz, dh, dw):
         return (lax.rem(z + dz + nz, nz), lax.rem(h + dh + nh, nh), lax.rem(w + dw, 2))
 
+    loads = [
+        pltpu.make_async_copy(source, target, load_sem.at[n])
+        for n, (source, target) in enumerate(((cl_hbm, cl), (w1_hbm, w1), (w2_hbm, w2)))
+    ]
+    for copy in loads:
+        copy.start()
+
+    heights = [(ox, oy) for ox in range(nx) for oy in range(ny)]
+    heights.sort(key=lambda place: -(min(place[0], nx - place[0]) + min(place[1], ny - place[1])))
+    targets_h = [lax.rem(hx + ox, nx) * ny + lax.rem(hy + oy, ny) for ox, oy in heights]
+
+    def for_each_device(act):
+        def step(n, _):
+            dz, dw = far_first(n // 2, nz), 1 - n % 2
+            zt, wt = lax.rem(z + dz, nz), lax.rem(w + dw, 2)
+            for ht in targets_h[:-1]:
+                act((zt, ht, wt))
+
+            @pl.when(n < 2 * nz - 1)
+            def _():
+                act((zt, h, wt))
+
+            return 0
+
+        lax.fori_loop(0, 2 * nz, step, 0)
+
+    devices = 2 * nz * nh
     barrier = pltpu.get_barrier_semaphore()
-    partners = [(dz, dh, dw) for dz in range(nz) for dh in (-1, 0, 1) for dw in range(2) if (dz, dh, dw) != (0, 0, 0)]
-    partners += [(0, dh, 0) for dh in range(2, nh - 1)]
-    for offset in partners:
-        pl.semaphore_signal(barrier, inc=1, device_id=dev(*offset), device_id_type=MESH)
-    pl.semaphore_wait(barrier, len(partners))
+    for_each_device(
+        lambda where: pl.semaphore_signal(barrier, inc=1, device_id=where, device_id_type=MESH)
+    )
+    pl.semaphore_wait(barrier, devices - 1)
+
+    def take(ref, sem):
+        pltpu.make_async_copy(ref, ref, sem).wait()
 
     def remote(src, dst, send, recv, where):
         return pltpu.make_async_remote_copy(
@@ -82,12 +126,9 @@
                 source = src.at[:, pl.ds(r_from, count), pl.ds(pl.multiple_of(q * strip, strip), strip), :]
                 target = dst.at[own_frames, pl.ds(r_to, count)]
                 if dz == 0 and dh == 0:
-                    copies.append(pltpu.make_async_copy(source, target, in_local.at[k, 0]))
+                    copies.append(pltpu.make_async_copy(source, target, in_recv.at[k, 0]))
                 else:
-                    place = dz * 3 + n
-                    copies.append(
-                        remote(source, target, in_send.at[k, place], in_recv.at[k, place], dev(dz, dh, 0))
-                    )
+                    copies.append(remote(source, target, in_send.at[k], in_recv.at[k, 0], dev(dz, dh, 0)))
         return copies
 
     def build_edges(src, edges):
@@ -113,19 +154,15 @@
 
     def edge_copies(k, edges, landing, landing_out):
         copies = []
-        base = 3 * nz
         for dz in range(nz):
             q = lax.rem(z + dz, nz)
             for n, dh in enumerate((0, 1, -1)):
                 source = edges.at[q]
                 target = landing.at[1 - dh, own_frames]
-                place = base + dz * 3 + n
                 if dz == 0 and dh == 0:
-                    copies.append(pltpu.make_async_copy(source, target, in_local.at[k, 1]))
+                    copies.append(pltpu.make_async_copy(source, target, in_recv.at[k, 1]))
                 else:
-                    copies.append(
-                        remote(source, target, in_send.at[k, place], in_recv.at[k, place], dev(dz, dh, 0))
-                    )
+                    copies.append(remote(source, target, in_send.at[k], in_recv.at[k, 1], dev(dz, dh, 0)))
         return copies
 
     outer_q = (nz - 1) * w
@@ -133,101 +170,63 @@
 
     def outer_sends(k, edges, landing_out):
         copies = []
-        base = 6 * nz
-        for n, dh in enumerate((0, 1, -1)):
+        for dh in (0, 1, -1):
             where = (outer_q, lax.rem(h + dh + nh, nh), 1 - w)
             copies.append(
-                remote(
-                    edges.at[nz], landing_out.at[1 - dh, own_frames],
-                    in_send.at[k, base + n], in_recv.at[k, base + 3 * z + n], where,
-                )
+                remote(edges.at[nz], landing_out.at[1 - dh, own_frames], in_send.at[k], in_recv.at[k, 2], where)
             )
         return copies
 
-    def outer_waits(k, edges, landing_out):
-        for zs in range(nz):
-            for n, dh in enumerate((0, 1, -1)):
-                remote(
-                    edges.at[nz], landing_out.at[1 - dh, pl.ds(zs * fl, fl)],
-                    in_send.at[k, 6 * nz + n], in_recv.at[k, 6 * nz + 3 * zs + n], dev(0, 0, 1),
-                ).wait_recv()
-
-    def wait_copies(copies):
+    def wait_inputs(k, cells_in, landing, landing_out):
+        take(cells_in, in_recv.at[k, 0])
+        take(landing, in_recv.at[k, 1])
+
+        @pl.when(takes_outer)
+        def _():
+            take(landing_out, in_recv.at[k, 2])
+
+    def start_all(copies):
         for copy in copies:
-            copy.wait()
+            copy.start()
+
+    def wait_sends(copies):
+        for copy in copies:
+            copy.wait_send()
 
     x_main = main_copies(0, xl, xr)
-    for copy in x_main:
-        copy.start()
+    start_all(x_main)
     build_edges(xl, xe)
     x_edge = edge_copies(0, xe, xeb, xex)
     x_outer = outer_sends(0, xe, xex)
-    for copy in x_edge + x_outer:
-        copy.start()
+    start_all(x_edge + x_outer)
+    loads[0].wait()
     c_main = main_copies(1, cl, cr)
-    for copy in c_main:
-        copy.start()
-
-    me8 = z * 2 + w
-
-    def red1_copies(k):
-        copies = []
-        for n, (dz, dw) in enumerate([(dz, dw) for dz in range(nz) for dw in range(2) if (dz, dw) != (0, 0)]):
-            slot = rb1.at[k, me8]
-            copies.append(remote(slot, slot, red_send.at[k, n], red_recv.at[k, n], dev(dz, 0, dw)))
-        return copies
-
-    def red2_copies(k):
-        copies = []
-        for dh in range(1, nh):
-            slot = rb2.at[k, h]
-            n = 2 * nz + dh
-            copies.append(remote(slot, slot, red_send.at[k, n], red_recv.at[k, n], dev(0, dh, 0)))
-        return copies
-
-    def start_all(copies):
-        for copy in copies:
-            copy.start()
-
-    def red1_start(k, tile):
-        rb1[k, me8] = tile
-        start_all(red1_copies(k))
-
-    def red2_start(k, tile):
-        rb2[k, h] = tile
-        start_all(red2_copies(k))
-
-    def moments(buffer, k, count, size):
-        mean = jnp.sum(buffer[k, :, 0:1, :], axis=0) / count
-        spread = jnp.zeros((1, CH), F32)
-        for n in range(count):
-            off = buffer[k, n, 0:1, :] - mean
-            spread = spread + (buffer[k, n, 1:2, :] + size * off * off)
-        return mean, spread
-
-    def plain_sums(buffer, k):
-        return jnp.sum(buffer[k], axis=0)
-
+    start_all(c_main)
+
+    me = (z * nh + h) * 2 + w
     local_size = 4.0 * fl * rl * cols
-    total_size = local_size * 2 * nz * nh
-
-    def moments_mid(k):
-        wait_copies(red1_copies(k))
-        mean, spread = moments(rb1, k, 2 * nz, local_size)
-        red2_start(k, tile_of(mean, spread))
+    total_size = local_size * devices
+
+    def red_start(k, first, second):
+        rb[k, me] = pack_pair(first, second)
+        slot = rb.at[k, me]
+        for_each_device(lambda where: remote(slot, slot, red_send.at[k], red_recv.at[k], where).start())
+
+    def red_wait(k):
+        take(rb.at[k, pl.ds(0, devices - 1)], red_recv.at[k])
 
     def moments_end(k):
-        wait_copies(red2_copies(k))
-        return moments(rb2, k, nh, local_size * 2 * nz)
-
-    def sums_mid(k):
-        wait_copies(red1_copies(k))
-        red2_start(k, plain_sums(rb1, k))
+        red_wait(k)
+        rows = rb[k]
+        mean, _ = unpack_pair(jnp.sum(rows, axis=0) / devices)
+        low = lanes_low(rows)
+        off = rows - jnp.where(lanes_low(mean), mean, 0.0)[None]
+        between, within = unpack_pair(jnp.sum(jnp.where(low, off * off, off), axis=0))
+        return mean, within + local_size * between
 
     def sums_end(k):
-        wait_copies(red2_copies(k))
-        sums = plain_sums(rb2, k) / total_size
-        return sums[0:1], sums[1:2]
+        red_wait(k)
+        return unpack_pair(jnp.sum(rb[k], axis=0) / total_size)
 
     zero8 = jnp.zeros((8, CH), F32)
 
@@ -241,13 +240,15 @@
         return total + fold_rows(off * off)
 
     local_spread = group_sum(total_row(lax.fori_loop(0, fl * rl, x_spread, zero8)))
-    red1_start(0, tile_of(local_mean, local_spread))
+    red_start(0, local_mean, local_spread)
 
     build_edges(cl, ce)
     c_edge = edge_copies(1, ce, ceb, cex)
     c_outer = outer_sends(1, ce, cex)
     start_all(c_edge + c_outer)
 
+    loads[1].wait()
+    loads[2].wait()
     for kt in range(3):
         for kr in range(3):
             for kc in range(3):
@@ -255,7 +256,6 @@
                 back = ((2 - kr) * 3 + (2 - kc)) * CH
                 for source, target in ((w1, wb1), (w2, wb2)):
                     target[back : back + CH, kt * CH : (kt + 1) * CH] = source[:, tap * CH : (tap + 1) * CH]
-    moments_mid(0)
     for kt in range(3):
         for kr in range(3):
             for kc in range(3):
@@ -329,7 +329,7 @@
     def window(stack, f):
         return [stack[f, kr : kr + rl].reshape(cells, 3 * CH) for kr in range(3)]
 
-    def convolve(stack, weight, target):
+    def convolve(stack, weight, target, first=0, last=None):
         def step(f, _):
             product = jnp.dot(
                 jnp.concatenate(window(stack, f), axis=1), weight[...], preferred_element_type=F32
@@ -338,7 +338,7 @@
                 target[f + j] += product[:, j * CH : (j + 1) * CH]
             return 0
 
-        lax.fori_loop(0, frames, step, 0)
+        lax.fori_loop(first, frames if last is None else last, step, 0)
 
     def weight_part(turned, stack, kr):
         left = jnp.concatenate([turned[f * CH : (f + 3) * CH, :] for f in range(frames)], axis=1)
@@ -359,14 +359,16 @@
     tiles = span * 9
     piece = -(-tiles // ns)
     outs = (o1_ref, o2_ref)
-    step_at = {"core": 0, "a1": 1, "a2": 1 + (ns - 1), "a3": 1 + 2 * (ns - 1), "g2": 1 + 3 * (ns - 1),
-               "g1": 1 + 4 * (ns - 1), "gc": 1 + 5 * (ns - 1)}
-
-    def sems(g, p, stage, n):
-        return ar_send.at[g, p, step_at[stage] + n], ar_recv.at[g, p, step_at[stage] + n]
+    stage_at = {"core": 0, "a1": 1, "a2": 2, "a3": 3, "g2": 4, "g1": 5, "gc": 6}
+
+    def sems(g, p, stage):
+        return ar_send.at[g], ar_recv.at[g, p, stage_at[stage]]
+
+    def arrived(g, p, stage, ref):
+        take(ref, ar_recv.at[g, p, stage_at[stage]])
 
     def core_copy(g, p):
-        return remote(a.at[g, p, pl.ds((1 - w) * half, half)], r0.at[g, p], *sems(g, p, "core", 0), dev(0, 0, 1))
+        return remote(a.at[g, p, pl.ds((1 - w) * half, half)], r0.at[g, p], *sems(g, p, "core"), dev(0, 0, 1))
 
     def core_start(g, p):
         core_copy(g, p).start()
@@ -376,13 +378,13 @@
         return [
             remote(
                 b1.at[g, p, pl.ds(lax.rem(coords[axis] + j, ns) * span, span)], r1.at[g, p, j - 1],
-                *sems(g, p, "a1", j - 1), peer(axis, j),
+                *sems(g, p, "a1"), peer(axis, j),
             )
             for j in range(1, ns)
         ]
 
     def a1_start(g, p):
-        core_copy(g, p).wait()
+        arrived(g, p, "core", r0.at[g, p])
         b1[g, p] = a[g, p, pl.ds(w * half, half)] + r0[g, p]
         start_all(a1_copies(g, p))
 
@@ -391,13 +393,13 @@
         return [
             remote(
                 b2.at[g, p, pl.ds(lax.rem(coords[axis] + j, ns) * piece, piece)], r2.at[g, p, j - 1],
-                *sems(g, p, "a2", j - 1), peer(axis, j),
+                *sems(g, p, "a2"), peer(axis, j),
             )
             for j in range(1, ns)
         ]
 
     def a2_start(g, p):
-        wait_copies(a1_copies(g, p))
+        arrived(g, p, "a1", r1.at[g, p])
         value = b1[g, p, pl.ds(coords[orders[p][0]] * span, span)]
         for j in range(ns - 1):
             value = value + r1[g, p, j]
@@ -409,10 +411,10 @@
     def a3_copies(g, p):
         axis = orders[p][2]
         slot = r3.at[g, p, coords[axis]]
-        return [remote(slot, slot, *sems(g, p, "a3", j - 1), peer(axis, j)) for j in range(1, ns)]
+        return [remote(slot, slot, *sems(g, p, "a3"), peer(axis, j)) for j in range(1, ns)]
 
     def a3_start(g, p):
-        wait_copies(a2_copies(g, p))
+        arrived(g, p, "a2", r2.at[g, p])
         value = b2[g, p, pl.ds(coords[orders[p][1]] * piece, piece)]
         for j in range(ns - 1):
             value = value + r2[g, p, j]
@@ -422,10 +424,10 @@
     def g2_copies(g, p):
         axis = orders[p][1]
         part = g3.at[g, p, pl.ds(coords[axis] * piece, piece)]
-        return [remote(part, part, *sems(g, p, "g2", j - 1), peer(axis, j)) for j in range(1, ns)]
+        return [remote(part, part, *sems(g, p, "g2"), peer(axis, j)) for j in range(1, ns)]
 
     def g2_start(g, p):
-        wait_copies(a3_copies(g, p))
+        arrived(g, p, "a3", r3.at[g, p, pl.ds(0, ns - 1)])
         value = r3[g, p, 0]
         for n in range(1, ns):
             value = value + r3[g, p, n]
@@ -438,33 +440,45 @@
     def g1_copies(g, p):
         axis = orders[p][0]
         part = out_span(g, p, coords[axis])
-        return [remote(part, part, *sems(g, p, "g1", j - 1), peer(axis, j)) for j in range(1, ns)]
+        return [remote(part, part, *sems(g, p, "g1"), peer(axis, j)) for j in range(1, ns)]
 
     def gc_copy(g, p, j):
         part = out_span(g, p, lax.rem(coords[orders[p][0]] + ns - j, ns))
-        return remote(part, part, *sems(g, p, "gc", j), dev(0, 0, 1))
+        return remote(part, part, *sems(g, p, "gc"), dev(0, 0, 1))
 
     def g1_start(g, p):
-        wait_copies(g2_copies(g, p))
+        arrived(g, p, "g2", g3.at[g, p, pl.ds(0, (ns - 1) * piece)])
         outs[g][p, pl.ds(w * half + coords[orders[p][0]] * span, span)] = g3[g, p, 0:tiles].reshape(span, 9, 8, CH)
         start_all(g1_copies(g, p))
         gc_copy(g, p, 0).start()
 
     def gc_start(g, p):
-        for j, copy in enumerate(g1_copies(g, p)):
-            copy.wait()
-            gc_copy(g, p, j + 1).start()
+        arrived(g, p, "g1", outs[g].at[p, pl.ds(0, (ns - 1) * span)])
+        for j in range(1, ns):
+            gc_copy(g, p, j).start()
+
+    def store_copy(g, p):
+        return pltpu.make_async_copy(outs[g].at[p], (o1_hbm, o2_hbm)[g].at[p], store_sem.at[1 + g])
 
     def gc_end(g, p):
-        for j in range(ns):
-            gc_copy(g, p, j).wait()
+        arrived(g, p, "gc", outs[g].at[p, pl.ds(0, half)])
+        store_copy(g, p).start()
+
+    def ar_close(g):
+        for p in range(3):
+            wait_sends([core_copy(g, p)] + a1_copies(g, p) + a2_copies(g, p) + a3_copies(g, p))
+            wait_sends(g2_copies(g, p) + g1_copies(g, p) + [gc_copy(g, p, j) for j in range(ns)])
 
     def each(stage, g):
         for p in range(3):
             stage(g, p)
 
     mean1, spread1 = moments_end(0)
-    scale = scale_ref[...]
+    picks = lax.broadcasted_iota(jnp.int32, (CH // 4, CH), 1) // 4 == lax.broadcasted_iota(jnp.int32, (CH // 4, CH), 0)
+    spread_exponent = jnp.dot(
+        jnp.broadcast_to(exponent_ref[...].astype(F32), (8, CH // 4)), picks.astype(F32), preferred_element_type=F32
+    )
+    scale = jnp.exp2(spread_exponent[0:1])
     inv1 = 1.0 / jnp.sqrt(spread1 * (scale * scale) / total_size + EPS)
     factor1 = scale * inv1
     gain1, shift1 = gain1_ref[...], shift1_ref[...]
@@ -477,14 +491,7 @@
         pre = (value - mean1) * factor1 * gain1 + shift1
         return rounded(pre * sigmoid(pre))
 
-    wait_copies(x_main + x_edge)
-    for copy in x_outer:
-        copy.wait_send()
-
-    @pl.when(takes_outer)
-    def _():
-        outer_waits(0, xe, xex)
-
+    wait_inputs(0, xr, xeb, xex)
     input_stack(s1, xr, xeb, xex, act_first)
     convolve(s1, wf1, hid)
 
@@ -497,18 +504,10 @@
         off = hid[n] - mean_l
         return total + fold_rows(off * off)
 
-    red1_start(1, tile_of(mean_l, group_sum(total_row(lax.fori_loop(0, frames, hid_spread, zero8)))))
-
-    wait_copies(c_main + c_edge)
-    for copy in c_outer:
-        copy.wait_send()
-
-    @pl.when(takes_outer)
-    def _():
-        outer_waits(1, ce, cex)
-
+    red_start(1, mean_l, group_sum(total_row(lax.fori_loop(0, frames, hid_spread, zero8))))
+
+    wait_inputs(1, cr, ceb, cex)
     input_stack(sc, cr, ceb, cex, lambda value: value)
-    moments_mid(1)
     convolve(sc, wb2, g2)
     mean2, spread2 = moments_end(1)
     inv2 = 1.0 / jnp.sqrt(spread2 / total_size + EPS)
@@ -525,7 +524,7 @@
         return first_total + fold_rows(scaled), second_total + fold_rows(scaled * normed)
 
     t1, t2 = lax.fori_loop(0, frames, second, (zero8, zero8))
-    red1_start(2, tile_of(group_sum(total_row(t1)), group_sum(total_row(t2))))
+    red_start(2, group_sum(total_row(t1)), group_sum(total_row(t2)))
 
     def put_second(kr):
         block = weight_part(act_t, sc, kr)
@@ -535,10 +534,9 @@
                 a[1, 2 - kr, :, kt * 3 + (2 - kc)] = part.reshape(16, 8, CH)
         core_start(1, 2 - kr)
 
-    put_second(0)
-    sums_mid(2)
-    put_second(1)
-    put_second(2)
+    for kr in range(3):
+        put_second(kr)
+    each(a1_start, 1)
     m1, m2 = sums_end(2)
 
     def hidden(n, _):
@@ -566,13 +564,12 @@
 
     halo = [
         remote(hg.at[:, pl.ds(rl, 1)], hg.at[:, pl.ds(0, 1)], halo_send.at[0], halo_recv.at[0], dev(0, 1, 0)),
-        remote(hg.at[:, pl.ds(1, 1)], hg.at[:, pl.ds(rl + 1, 1)], halo_send.at[1], halo_recv.at[1], dev(0, -1, 0)),
+        remote(hg.at[:, pl.ds(1, 1)], hg.at[:, pl.ds(rl + 1, 1)], halo_send.at[0], halo_recv.at[0], dev(0, -1, 0)),
     ]
     for n, dh in enumerate((0, 1, -1)):
-        halo.append(remote(eh.at[0], heb.at[1 - dh, 1], halo_send.at[2 + n], halo_recv.at[2 + n], beside(-1, dh)))
-        halo.append(remote(eh.at[1], heb.at[1 - dh, 0], halo_send.at[5 + n], halo_recv.at[5 + n], beside(1, dh)))
+        halo.append(remote(eh.at[0], heb.at[1 - dh, 1], halo_send.at[0], halo_recv.at[1], beside(-1, dh)))
+        halo.append(remote(eh.at[1], heb.at[1 - dh, 0], halo_send.at[0], halo_recv.at[1], beside(1, dh)))
     start_all(halo)
-    each(a1_start, 1)
 
     def put_first(kr):
         block = weight_part(hg_t, s1, kr)
@@ -584,7 +581,9 @@
 
     for kr in range(3):
         put_first(kr)
-    wait_copies(halo)
+    each(a1_start, 0)
+    take(hg.at[:, pl.ds(0, 2)], halo_recv.at[0])
+    take(heb, halo_recv.at[1])
 
     def halo_stack(f, _):
         lefts = [heb[d, 0, f].astype(F32) for d in range(3)]
@@ -596,10 +595,10 @@
 
     lax.fori_loop(0, frames, halo_stack, 0)
     each(a2_start, 1)
-    each(a1_start, 0)
-    convolve(sh, wb1, g1)
+    convolve(sh, wb1, g1, 0, frames // 2)
+    each(a2_start, 0)
+    convolve(sh, wb1, g1, frames // 2, frames)
     each(a3_start, 1)
-    each(a2_start, 0)
 
     def first(f, totals):
         first_total, second_total = totals
@@ -614,7 +613,7 @@
         return first_total, second_total
 
     t1, t2 = lax.fori_loop(0, frames, first, (zero8, zero8))
-    red1_start(3, tile_of(group_sum(total_row(t1)), group_sum(total_row(t2))))
+    red_start(3, group_sum(total_row(t1)), group_sum(total_row(t2)))
 
     back_copies = []
     for dz in range(nz):
@@ -622,30 +621,46 @@
         source = s_out.at[pl.ds(q * fl, fl)]
         target = s_in.at[:, :, pl.ds(pl.multiple_of(z * strip, strip), strip), :]
         if dz == 0:
-            back_copies.append(pltpu.make_async_copy(source, target, back_local.at[0]))
+            back_copies.append(pltpu.make_async_copy(source, target, back_recv.at[0]))
         else:
-            back_copies.append(remote(source, target, back_send.at[dz], back_recv.at[dz], dev(dz, 0, 0)))
+            back_copies.append(remote(source, target, back_send.at[0], back_recv.at[0], dev(dz, 0, 0)))
     start_all(back_copies)
+    each(a3_start, 0)
     each(g2_start, 1)
-    each(a3_start, 0)
-    sums_mid(3)
+    each(g2_start, 0)
     each(g1_start, 1)
-    each(g2_start, 0)
     m1, m2 = sums_end(3)
-    wait_copies(back_copies)
+    take(s_in, back_recv.at[0])
+
+    def out_copy(f):
+        return pltpu.make_async_copy(out_ref.at[f], out_hbm.at[f], store_sem.at[0])
+
+    for f in range(fl):
+
+        def last(r, _):
+            normed = (xl[f, r].astype(F32) - mean1) * factor1
+            out_ref[f, r] = cl[f, r].astype(F32) + inv1 * (s_in[f, r].astype(F32) - m1 - normed * m2)
+            return 0
+
+        lax.fori_loop(0, rl, last, 0)
+        out_copy(f).start()
     each(g1_start, 0)
-
-    def last(n, _):
-        f, r = n // rl, n % rl
-        normed = (xl[f, r].astype(F32) - mean1) * factor1
-        out_ref[f, r] = cl[f, r].astype(F32) + inv1 * (s_in[f, r].astype(F32) - m1 - normed * m2)
-        return 0
-
-    lax.fori_loop(0, fl * rl, last, 0)
     each(gc_start, 1)
+    each(gc_end, 1)
+    wait_sends(x_main[1:] + x_edge[1:] + x_outer)
+    wait_sends(c_main[1:] + c_edge[1:] + c_outer)
+    for k in range(4):
+        take(rb.at[k, pl.ds(0, devices - 1)], red_send.at[k])
+    wait_sends(halo + back_copies[1:])
+    ar_close(1)
     each(gc_start, 0)
-    each(gc_end, 1)
     each(gc_end, 0)
+    ar_close(0)
+    for f in range(fl):
+        out_copy(f).wait()
+    for g in range(2):
+        for p in range(3):
+            store_copy(g, p).wait()
 
 
 def shards(sizes, latent, exponents, cotangent, conv_first, conv_second, gain_first, shift_first, gain_second, shift_second):
@@ -658,14 +673,19 @@
     span = 8 // ns
     tiles = span * 9
     piece = -(-tiles // ns)
-    scale = jnp.repeat(jnp.exp2(exponents.astype(F32)), channels // exponents.shape[0])[None]
     xl = jnp.transpose(latent, (1, 2, 3, 0))
     cl = jnp.transpose(cotangent, (1, 2, 3, 0))
     vmem = pl.BlockSpec(memory_space=pltpu.VMEM)
-    n_ar = 1 + 5 * (ns - 1) + ns
-    n_in = 6 * nz + 3 * nz
+    any_space = pl.BlockSpec(memory_space=pl.ANY)
+    part = (3, 16, 9, 8, CH)
     wide = (frames, rl + 2, strip, 3 * CH)
     scratch = [
+        pltpu.VMEM((fl, rl, cols, CH), BF16),
+        pltpu.VMEM((CH, 27 * CH), BF16),
+        pltpu.VMEM((CH, 27 * CH), BF16),
+        pltpu.VMEM((fl, rl, cols, CH), F32),
+        pltpu.VMEM(part, F32),
+        pltpu.VMEM(part, F32),
         pltpu.VMEM((frames, rl + 2, strip, CH), BF16),
         pltpu.VMEM((frames, rl + 2, strip, CH), BF16),
         pltpu.VMEM((nz + 1, fl, 16, CH), BF16),
@@ -689,11 +709,9 @@
         pltpu.VMEM((9 * CH, 3 * CH), BF16),
         pltpu.VMEM((9 * CH, 3 * CH), BF16),
         pltpu.VMEM((9 * CH, 3 * CH), BF16),
-        pltpu.VMEM((8, CH), F32),
         pltpu.VMEM((frames, rl, strip, CH), BF16),
         pltpu.VMEM((fl, rl, cols, CH), BF16),
-        pltpu.VMEM((4, 2 * nz, 8, CH), F32),
-        pltpu.VMEM((4, nh, 8, CH), F32),
+        pltpu.VMEM((4, 2 * nz * nh, 1, CH), F32),
         pltpu.VMEM((2, 3, 16, 9, 8, CH), F32),
         pltpu.VMEM((2, 3, 8, 9, 8, CH), F32),
         pltpu.VMEM((2, 3, 8, 9, 8, CH), F32),
@@ -702,34 +720,34 @@
         pltpu.VMEM((2, 3, ns - 1, piece, 8, CH), F32),
         pltpu.VMEM((2, 3, ns, piece, 8, CH), F32),
         pltpu.VMEM((2, 3, piece * ns, 8, CH), F32),
-        pltpu.SemaphoreType.DMA((2, n_in)),
-        pltpu.SemaphoreType.DMA((2, n_in)),
-        pltpu.SemaphoreType.DMA((2, 2)),
-        pltpu.SemaphoreType.DMA((4, 2 * nz + nh)),
-        pltpu.SemaphoreType.DMA((4, 2 * nz + nh)),
-        pltpu.SemaphoreType.DMA((8,)),
-        pltpu.SemaphoreType.DMA((8,)),
-        pltpu.SemaphoreType.DMA((nz,)),
-        pltpu.SemaphoreType.DMA((nz,)),
+        pltpu.SemaphoreType.DMA((3,)),
+        pltpu.SemaphoreType.DMA((3,)),
+        pltpu.SemaphoreType.DMA((2,)),
+        pltpu.SemaphoreType.DMA((2, 3)),
+        pltpu.SemaphoreType.DMA((4,)),
+        pltpu.SemaphoreType.DMA((4,)),
         pltpu.SemaphoreType.DMA((1,)),
-        pltpu.SemaphoreType.DMA((2, 3, n_ar)),
-        pltpu.SemaphoreType.DMA((2, 3, n_ar)),
+        pltpu.SemaphoreType.DMA((2,)),
+        pltpu.SemaphoreType.DMA((1,)),
+        pltpu.SemaphoreType.DMA((1,)),
+        pltpu.SemaphoreType.DMA((2,)),
+        pltpu.SemaphoreType.DMA((2, 3, 7)),
     ]
     grad, first, second = pl.pallas_call(
         functools.partial(body, sizes),
         out_shape=(
             jax.ShapeDtypeStruct((fl, rl, cols, CH), F32),
-            jax.ShapeDtypeStruct((3, 16, 9, 8, CH), F32),
-            jax.ShapeDtypeStruct((3, 16, 9, 8, CH), F32),
+            jax.ShapeDtypeStruct(part, F32),
+            jax.ShapeDtypeStruct(part, F32),
         ),
-        in_specs=[vmem] * 9,
-        out_specs=(vmem, vmem, vmem),
+        in_specs=[vmem] + [any_space] * 3 + [vmem] * 5,
+        out_specs=(any_space,) * 3,
         scratch_shapes=scratch,
         compiler_params=pltpu.CompilerParams(
             collective_id=0, has_side_effects=True, vmem_limit_bytes=60 * 1024 * 1024
         ),
     )(
-        xl, cl, conv_first, conv_second, scale,
+        xl, cl, conv_first, conv_second, exponents[None],
         gain_first[None], shift_first[None], gain_second[None], shift_second[None],
     )
     first = first.reshape(3, 16, 3, 3, 8, CH).transpose(1, 4, 2, 0, 3, 5).reshape(CH, 27 * CH)

time: 124 us -> 108 us (0.87)
  Pallas kernels: 110 us -> 95.6 us
    pallas_call x1, Pallas kernels: 110 us -> 95.6 us  [shards(): pl.pallas_call(functools.partial(body, sizes), out_shape=(jax.ShapeDtypeS...]
where the time goes in v2:
time: 108 us
  Pallas kernels  95.6 us (89%)
  local copies, waits for them, and re-layouts  11.4 us (11%)
    pallas_call x1, Pallas kernels, shards(): pl.pallas_call(functools.partial(body, sizes), out_shape=(jax.ShapeDtypeS...  95.6 us
    unnamed x8, local copies, waits for them, and re-layouts  9.9 us

profile of v2, /device:TPU:1, one launch (start us, length us, event | category | flops | bytes accessed | tf_op | source)
XLA Modules:
  0.0 107.7 jit_solution(3666338494336789977)
XLA Ops:
  0.6 2.2 %copy.17 = bf16[128,2,4,256]{0,3,2,1:T(8,128)(2,1)} copy(bf16[128,2,4,256]{3,2,1,0:T(4,128)(2,1)} %param.9) | data formatting | bytes 1048576 | tf_op args[0]
  2.9 2.2 %copy.18 = bf16[128,2,4,256]{0,3,2,1:T(8,128)(2,1)} copy(bf16[128,2,4,256]{3,2,1,0:T(4,128)(2,1)} %param.11) | data formatting | bytes 1048576 | tf_op args[2]
  5.1 95.6 %shard_map.112 = (f32[2,4,256,128]{3,2,1,0:T(8,128)}, f32[3,16,9,8,128]{4,3,2,1,0:T(8,128)}, f32[3,16,9,8,128]{4,3,2,1,0:T(8,128)}) custom-call(bf16[2,4,256,128]{3,2,1,0:T(8,128)(2,1)} %bitcast.17, bf16[2,4,256,128]{3,2,1,0:T(8,128)(2,1)} %bitcast.18, bf16[128,3456]{1,0:T(8,128)(2,1)} %w1_hbm.1, bf16[128,3456]{1,0:T(8,128)(2,1)} %w2_hbm.1, ...), custom_call_target="tpu_custom_call" | custom-call | tf_op jit(solution)/shard_map/pallas_call | solution.py:736
  100.7 0.0 copy-start.1
  100.7 2.7 %copy.21 = f32[128,2,4,256]{3,2,1,0:T(4,128)} copy(f32[128,2,4,256]{0,3,2,1:T(8,128)} %bitcast.22) | data formatting | bytes 2097152
  103.4 0.0 copy-done.1
  103.4 0.0 copy-start
  103.4 1.3 %copy.19 = f32[16,8,3,3,3,128]{5,1,4,3,2,0:T(8,128)} copy(f32[16,8,3,3,3,128]{5,1,4,2,0,3:T(8,128)S(1)} %bitcast.21) | data formatting | bytes 3538944 | tf_op jit(solution)/shard_map/transpose | solution.py:753
  104.8 0.8 copy-done
  105.5 0.2 copy.20
  105.8 1.9 %copy.22 = f32[128,3456]{1,0:T(8,128)} copy(f32[128,3456]{0,1:T(8,128)S(1)} %bitcast.16) | data formatting | bytes 3538944
Async XLA Ops:
  100.7 2.7 %copy-start.1 = (f32[3,16,9,8,128]{4,3,2,1,0:T(8,128)S(1)}, f32[3,16,9,8,128]{4,3,2,1,0:T(8,128)}, u32[]{:S(2)}) copy-start(f32[3,16,9,8,128]{4,3,2,1,0:T(8,128)} %get-tuple-element.7) | copy-start | bytes 5308420
  103.4 2.1 %copy-start = (f32[3,16,9,8,128]{4,3,2,1,0:T(8,128)S(1)}, f32[3,16,9,8,128]{4,3,2,1,0:T(8,128)}, u32[]{:S(2)}) copy-start(f32[3,16,9,8,128]{4,3,2,1,0:T(8,128)} %get-tuple-element.8) | copy-start | bytes 5308420

commit v3 on v2

--- a/solution.py
+++ b/solution.py
@@ -53,9 +53,9 @@
 
 def body(
     sizes,
-    xl, cl_hbm, w1_hbm, w2_hbm, exponent_ref, gain1_ref, shift1_ref, gain2_ref, shift2_ref,
+    x_hbm, c_hbm, w1_hbm, w2_hbm, exponent_ref, gain1_ref, shift1_ref, gain2_ref, shift2_ref,
     out_hbm, o1_hbm, o2_hbm,
-    cl, w1, w2, out_ref, o1_ref, o2_ref,
+    x_raw, c_raw, xl, cl, w1, w2, out_ref, o1_ref, o2_ref, fin1, fin2,
     xr, cr, xe, ce, xeb, ceb, xex, cex, s1, sc, sh, hid, g2, g1, nrm, act_t, hg_t, hg, eh, heb,
     wf1, wb1, wb2, s_out, s_in, rb, a, r0, b1, r1, b2, r2, r3, g3,
     load_sem, store_sem, in_send, in_recv, red_send, red_recv, halo_send, halo_recv, back_send, back_recv,
@@ -75,7 +75,7 @@
 
     loads = [
         pltpu.make_async_copy(source, target, load_sem.at[n])
-        for n, (source, target) in enumerate(((cl_hbm, cl), (w1_hbm, w1), (w2_hbm, w2)))
+        for n, (source, target) in enumerate(((x_hbm, x_raw), (c_hbm, c_raw), (w1_hbm, w1), (w2_hbm, w2)))
     ]
     for copy in loads:
         copy.start()
@@ -101,10 +101,11 @@
 
     devices = 2 * nz * nh
     barrier = pltpu.get_barrier_semaphore()
-    for_each_device(
-        lambda where: pl.semaphore_signal(barrier, inc=1, device_id=where, device_id_type=MESH)
-    )
-    pl.semaphore_wait(barrier, devices - 1)
+    for dz in reversed(range(nz)):
+        for dw in (1, 0):
+            zt, wt = lax.rem(z + dz, nz), lax.rem(w + dw, 2)
+            for ht in targets_h if (dz, dw) != (0, 0) else targets_h[:-1]:
+                pl.semaphore_signal(barrier, inc=1, device_id=(zt, ht, wt), device_id_type=MESH)
 
     def take(ref, sem):
         pltpu.make_async_copy(ref, ref, sem).wait()
@@ -193,16 +194,6 @@
         for copy in copies:
             copy.wait_send()
 
-    x_main = main_copies(0, xl, xr)
-    start_all(x_main)
-    build_edges(xl, xe)
-    x_edge = edge_copies(0, xe, xeb, xex)
-    x_outer = outer_sends(0, xe, xex)
-    start_all(x_edge + x_outer)
-    loads[0].wait()
-    c_main = main_copies(1, cl, cr)
-    start_all(c_main)
-
     me = (z * nh + h) * 2 + w
     local_size = 4.0 * fl * rl * cols
     total_size = local_size * devices
@@ -228,6 +219,14 @@
         red_wait(k)
         return unpack_pair(jnp.sum(rb[k], axis=0) / total_size)
 
+    def turn(source, target):
+        for f in range(fl):
+            for r in range(rl):
+                target[f, r] = jnp.transpose(source[:, f, r, :].astype(F32)).astype(BF16)
+
+    loads[0].wait()
+    turn(x_raw, xl)
+    build_edges(xl, xe)
     zero8 = jnp.zeros((8, CH), F32)
 
     def x_sum(n, total):
@@ -240,15 +239,12 @@
         return total + fold_rows(off * off)
 
     local_spread = group_sum(total_row(lax.fori_loop(0, fl * rl, x_spread, zero8)))
-    red_start(0, local_mean, local_spread)
-
+
+    loads[1].wait()
+    turn(c_raw, cl)
     build_edges(cl, ce)
-    c_edge = edge_copies(1, ce, ceb, cex)
-    c_outer = outer_sends(1, ce, cex)
-    start_all(c_edge + c_outer)
-
-    loads[1].wait()
     loads[2].wait()
+    loads[3].wait()
     for kt in range(3):
         for kr in range(3):
             for kc in range(3):
@@ -263,6 +259,16 @@
                 ahead = (kr * 3 + kc) * CH
                 block = w1[:, tap * CH : (tap + 1) * CH].astype(F32)
                 wf1[ahead : ahead + CH, (2 - kt) * CH : (3 - kt) * CH] = jnp.transpose(block).astype(BF16)
+    pl.semaphore_wait(barrier, devices - 1)
+    x_main = main_copies(0, xl, xr)
+    x_edge = edge_copies(0, xe, xeb, xex)
+    x_outer = outer_sends(0, xe, xex)
+    start_all(x_main + x_edge + x_outer)
+    red_start(0, local_mean, local_spread)
+    c_main = main_copies(1, cl, cr)
+    c_edge = edge_copies(1, ce, ceb, cex)
+    c_outer = outer_sends(1, ce, cex)
+    start_all(c_main + c_edge + c_outer)
     zero_cells = jnp.zeros((cells, CH), F32)
 
     def clear(n, _):
@@ -457,12 +463,16 @@
         for j in range(1, ns):
             gc_copy(g, p, j).start()
 
-    def store_copy(g, p):
-        return pltpu.make_async_copy(outs[g].at[p], (o1_hbm, o2_hbm)[g].at[p], store_sem.at[1 + g])
+    def store_copy(g):
+        return pltpu.make_async_copy((fin1, fin2)[g], (o1_hbm, o2_hbm)[g], store_sem.at[1 + g])
 
     def gc_end(g, p):
         arrived(g, p, "gc", outs[g].at[p, pl.ds(0, half)])
-        store_copy(g, p).start()
+        for kt in range(3):
+            for kc in range(3):
+                block = outs[g][p, :, kt * 3 + kc].reshape(CH, CH)
+                tap = 9 * kt + 3 * p + kc
+                (fin1, fin2)[g][:, tap * CH : (tap + 1) * CH] = block if g == 0 else jnp.transpose(block)
 
     def ar_close(g):
         for p in range(3):
@@ -595,10 +605,6 @@
 
     lax.fori_loop(0, frames, halo_stack, 0)
     each(a2_start, 1)
-    convolve(sh, wb1, g1, 0, frames // 2)
-    each(a2_start, 0)
-    convolve(sh, wb1, g1, frames // 2, frames)
-    each(a3_start, 1)
 
     def first(f, totals):
         first_total, second_total = totals
@@ -612,19 +618,34 @@
             second_total = second_total + fold_rows(scaled * normed)
         return first_total, second_total
 
-    t1, t2 = lax.fori_loop(0, frames, first, (zero8, zero8))
+    back_from = s_in.at[:, :, pl.ds(pl.multiple_of(z * strip, strip), strip), :]
+    back_copies = []
+
+    def send_back(q):
+        source = s_out.at[pl.ds(q * fl, fl)]
+        far = remote(source, back_from, back_send.at[0], back_recv.at[0], (q, h, w))
+        back_copies.append(far)
+
+        @pl.when(z == q)
+        def _():
+            pltpu.make_async_copy(source, back_from, back_recv.at[0]).start()
+
+        @pl.when(z != q)
+        def _():
+            far.start()
+
+    convolve(sh, wb1, g1, 0, 2)
+    totals = (zero8, zero8)
+    for q in range(nz):
+        if q * fl + 2 < frames:
+            convolve(sh, wb1, g1, q * fl + 2, q * fl + fl + 2)
+        totals = lax.fori_loop(q * fl, q * fl + fl, first, totals)
+        send_back(q)
+        if q == nz // 2 - 1:
+            each(a2_start, 0)
+    t1, t2 = totals
     red_start(3, group_sum(total_row(t1)), group_sum(total_row(t2)))
-
-    back_copies = []
-    for dz in range(nz):
-        q = lax.rem(z + dz, nz)
-        source = s_out.at[pl.ds(q * fl, fl)]
-        target = s_in.at[:, :, pl.ds(pl.multiple_of(z * strip, strip), strip), :]
-        if dz == 0:
-            back_copies.append(pltpu.make_async_copy(source, target, back_recv.at[0]))
-        else:
-            back_copies.append(remote(source, target, back_send.at[0], back_recv.at[0], dev(dz, 0, 0)))
-    start_all(back_copies)
+    each(a3_start, 1)
     each(a3_start, 0)
     each(g2_start, 1)
     each(g2_start, 0)
@@ -633,34 +654,38 @@
     take(s_in, back_recv.at[0])
 
     def out_copy(f):
-        return pltpu.make_async_copy(out_ref.at[f], out_hbm.at[f], store_sem.at[0])
+        return pltpu.make_async_copy(out_ref.at[:, f], out_hbm.at[:, f], store_sem.at[0])
 
     for f in range(fl):
-
-        def last(r, _):
+        for r in range(rl):
             normed = (xl[f, r].astype(F32) - mean1) * factor1
-            out_ref[f, r] = cl[f, r].astype(F32) + inv1 * (s_in[f, r].astype(F32) - m1 - normed * m2)
-            return 0
-
-        lax.fori_loop(0, rl, last, 0)
+            value = cl[f, r].astype(F32) + inv1 * (s_in[f, r].astype(F32) - m1 - normed * m2)
+            out_ref[:, f, r, :] = jnp.transpose(value)
         out_copy(f).start()
     each(g1_start, 0)
     each(gc_start, 1)
     each(gc_end, 1)
+    store_copy(1).start()
     wait_sends(x_main[1:] + x_edge[1:] + x_outer)
     wait_sends(c_main[1:] + c_edge[1:] + c_outer)
     for k in range(4):
         take(rb.at[k, pl.ds(0, devices - 1)], red_send.at[k])
-    wait_sends(halo + back_copies[1:])
+    wait_sends(halo)
+    for q in range(nz):
+
+        @pl.when(z != q)
+        def _():
+            back_copies[q].wait_send()
+
     ar_close(1)
     each(gc_start, 0)
     each(gc_end, 0)
+    store_copy(0).start()
     ar_close(0)
     for f in range(fl):
         out_copy(f).wait()
-    for g in range(2):
-        for p in range(3):
-            store_copy(g, p).wait()
+    store_copy(0).wait()
+    store_copy(1).wait()
 
 
 def shards(sizes, latent, exponents, cotangent, conv_first, conv_second, gain_first, shift_first, gain_second, shift_second):
@@ -673,19 +698,22 @@
     span = 8 // ns
     tiles = span * 9
     piece = -(-tiles // ns)
-    xl = jnp.transpose(latent, (1, 2, 3, 0))
-    cl = jnp.transpose(cotangent, (1, 2, 3, 0))
     vmem = pl.BlockSpec(memory_space=pltpu.VMEM)
     any_space = pl.BlockSpec(memory_space=pl.ANY)
     part = (3, 16, 9, 8, CH)
     wide = (frames, rl + 2, strip, 3 * CH)
     scratch = [
+        pltpu.VMEM((CH, fl, rl, cols), BF16),
+        pltpu.VMEM((CH, fl, rl, cols), BF16),
+        pltpu.VMEM((fl, rl, cols, CH), BF16),
         pltpu.VMEM((fl, rl, cols, CH), BF16),
         pltpu.VMEM((CH, 27 * CH), BF16),
         pltpu.VMEM((CH, 27 * CH), BF16),
-        pltpu.VMEM((fl, rl, cols, CH), F32),
+        pltpu.VMEM((CH, fl, rl, cols), F32),
         pltpu.VMEM(part, F32),
         pltpu.VMEM(part, F32),
+        pltpu.VMEM((CH, 27 * CH), F32),
+        pltpu.VMEM((CH, 27 * CH), F32),
         pltpu.VMEM((frames, rl + 2, strip, CH), BF16),
         pltpu.VMEM((frames, rl + 2, strip, CH), BF16),
         pltpu.VMEM((nz + 1, fl, 16, CH), BF16),
@@ -720,7 +748,7 @@
         pltpu.VMEM((2, 3, ns - 1, piece, 8, CH), F32),
         pltpu.VMEM((2, 3, ns, piece, 8, CH), F32),
         pltpu.VMEM((2, 3, piece * ns, 8, CH), F32),
-        pltpu.SemaphoreType.DMA((3,)),
+        pltpu.SemaphoreType.DMA((4,)),
         pltpu.SemaphoreType.DMA((3,)),
         pltpu.SemaphoreType.DMA((2,)),
         pltpu.SemaphoreType.DMA((2, 3)),
@@ -733,26 +761,23 @@
         pltpu.SemaphoreType.DMA((2,)),
         pltpu.SemaphoreType.DMA((2, 3, 7)),
     ]
-    grad, first, second = pl.pallas_call(
+    return pl.pallas_call(
         functools.partial(body, sizes),
         out_shape=(
-            jax.ShapeDtypeStruct((fl, rl, cols, CH), F32),
-            jax.ShapeDtypeStruct(part, F32),
-            jax.ShapeDtypeStruct(part, F32),
+            jax.ShapeDtypeStruct((CH, fl, rl, cols), F32),
+            jax.ShapeDtypeStruct((CH, 27 * CH), F32),
+            jax.ShapeDtypeStruct((CH, 27 * CH), F32),
         ),
-        in_specs=[vmem] + [any_space] * 3 + [vmem] * 5,
+        in_specs=[any_space] * 4 + [vmem] * 5,
         out_specs=(any_space,) * 3,
         scratch_shapes=scratch,
         compiler_params=pltpu.CompilerParams(
             collective_id=0, has_side_effects=True, vmem_limit_bytes=60 * 1024 * 1024
         ),
     )(
-        xl, cl, conv_first, conv_second, exponents[None],
+        latent, cotangent, conv_first, conv_second, exponents[None],
         gain_first[None], shift_first[None], gain_second[None], shift_second[None],
     )
-    first = first.reshape(3, 16, 3, 3, 8, CH).transpose(1, 4, 2, 0, 3, 5).reshape(CH, 27 * CH)
-    second = second.reshape(3, 16, 3, 3, 8, CH).transpose(5, 2, 0, 3, 1, 4).reshape(CH, 27 * CH)
-    return jnp.transpose(grad, (3, 0, 1, 2)), first, second
 
 
 def solution(mesh):

time: 108 us -> 97.3 us (0.901)
  local copies, waits for them, and re-layouts: 11.4 us -> 5.77 us
  Pallas kernels: 95.6 us -> 90.7 us
    pallas_call x1, Pallas kernels: 95.6 us -> 90.7 us  [shards(): pl.pallas_call(functools.partial(body, sizes), out_shape=(jax.ShapeDtypeS...]
    unnamed x8 -> x7, local copies, waits for them, and re-layouts: 9.9 us -> 5.77 us
    transpose x1 -> x0, local copies, waits for them, and re-layouts: 1.32 us -> none  [shards(): first.reshape(3, 16, 3, 3, 8, CH).transpose(1, 4, 2, 0, 3, 5)]
where the time goes in v3:
time: 97.3 us; the launch traced here: 97.1 us
  Pallas kernels  90.7 us (93%)
  local copies, waits for them, and re-layouts  5.77 us (6%)
    pallas_call x1, Pallas kernels, shards(): pl.pallas_call(functools.partial(body, sizes), out_shape=(jax.ShapeDtypeS...  90.7 us
    unnamed x7, local copies, waits for them, and re-layouts  5.77 us

profile of v3, /device:TPU:1, one launch (start us, length us, event | category | flops | bytes accessed | tf_op | source)
XLA Modules:
  0.0 97.1 jit_solution(15333011525475587707)
XLA Ops:
  0.6 90.7 %shard_map.112 = (f32[128,2,4,256]{3,2,1,0:T(4,128)}, f32[128,3456]{1,0:T(8,128)}, f32[128,3456]{1,0:T(8,128)}) custom-call(bf16[128,2,4,256]{3,2,1,0:T(4,128)(2,1)} %x_hbm.1, bf16[128,2,4,256]{3,2,1,0:T(4,128)(2,1)} %c_hbm.1, bf16[128,3456]{1,0:T(8,128)(2,1)} %w1_hbm.1, bf16[128,3456]{1,0:T(8,128)(2,1)} %w2_hbm.1, s32[1,32]{1,0:T(1,128)} %bitcast.5, ...), custom_call_target="tpu_custom_call" | custom-call | tf_op jit(solution)/shard_map/pallas_call | solution.py:764
  91.3 0.0 copy-start.1
  91.3 2.4 %copy.15 = f32[128,2,4,256]{3,2,1,0:T(4,128)} copy(f32[128,2,4,256]{3,2,1,0:T(4,128)} %get-tuple-element.6) | data formatting | bytes 2097152
  93.8 0.0 copy-done.1
  93.8 0.0 copy-start
  93.8 1.2 %copy.16 = f32[128,3456]{1,0:T(8,128)} copy(f32[128,3456]{1,0:T(8,128)S(1)} %copy-done.1) | data formatting | bytes 3538944
  95.0 0.9 copy-done
  95.9 1.2 %copy.17 = f32[128,3456]{1,0:T(8,128)} copy(f32[128,3456]{1,0:T(8,128)S(1)} %copy-done) | data formatting | bytes 3538944
Async XLA Ops:
  91.3 2.5 %copy-start.1 = (f32[128,3456]{1,0:T(8,128)S(1)}, f32[128,3456]{1,0:T(8,128)}, u32[]{:S(2)}) copy-start(f32[128,3456]{1,0:T(8,128)} %get-tuple-element.7) | copy-start | bytes 5308420
  93.8 2.1 %copy-start = (f32[128,3456]{1,0:T(8,128)S(1)}, f32[128,3456]{1,0:T(8,128)}, u32[]{:S(2)}) copy-start(f32[128,3456]{1,0:T(8,128)} %get-tuple-element.8) | copy-start | bytes 5308420

commit v4 on v3

--- a/solution.py
+++ b/solution.py
@@ -129,7 +129,7 @@
                 if dz == 0 and dh == 0:
                     copies.append(pltpu.make_async_copy(source, target, in_recv.at[k, 0]))
                 else:
-                    copies.append(remote(source, target, in_send.at[k], in_recv.at[k, 0], dev(dz, dh, 0)))
+                    copies.append(remote(source, target, in_send.at[k], in_recv.at[k, dz], dev(dz, dh, 0)))
         return copies
 
     def build_edges(src, edges):
@@ -161,9 +161,9 @@
                 source = edges.at[q]
                 target = landing.at[1 - dh, own_frames]
                 if dz == 0 and dh == 0:
-                    copies.append(pltpu.make_async_copy(source, target, in_recv.at[k, 1]))
+                    copies.append(pltpu.make_async_copy(source, target, in_recv.at[k, nz]))
                 else:
-                    copies.append(remote(source, target, in_send.at[k], in_recv.at[k, 1], dev(dz, dh, 0)))
+                    copies.append(remote(source, target, in_send.at[k], in_recv.at[k, nz + dz], dev(dz, dh, 0)))
         return copies
 
     outer_q = (nz - 1) * w
@@ -171,20 +171,25 @@
 
     def outer_sends(k, edges, landing_out):
         copies = []
+        recv = in_recv.at[k, 2 * nz + lax.rem(outer_q - z + nz, nz)]
         for dh in (0, 1, -1):
             where = (outer_q, lax.rem(h + dh + nh, nh), 1 - w)
-            copies.append(
-                remote(edges.at[nz], landing_out.at[1 - dh, own_frames], in_send.at[k], in_recv.at[k, 2], where)
-            )
+            copies.append(remote(edges.at[nz], landing_out.at[1 - dh, own_frames], in_send.at[k], recv, where))
         return copies
 
-    def wait_inputs(k, cells_in, landing, landing_out):
-        take(cells_in, in_recv.at[k, 0])
-        take(landing, in_recv.at[k, 1])
+    near_first = sorted(range(nz), key=lambda dz: min(dz, nz - dz))
+
+    def pair_from(dz):
+        return lax.rem(z - dz + nz, nz) * fl
+
+    def wait_pair(k, dz, cells_in, landing, landing_out):
+        pair = pl.ds(pair_from(dz), fl)
+        take(cells_in.at[pair], in_recv.at[k, dz])
+        take(landing.at[:, pair], in_recv.at[k, nz + dz])
 
         @pl.when(takes_outer)
         def _():
-            take(landing_out, in_recv.at[k, 2])
+            take(landing_out.at[:, pair], in_recv.at[k, 2 * nz + dz])
 
     def start_all(copies):
         for copy in copies:
@@ -315,7 +320,7 @@
     edge_place = lax.broadcasted_iota(jnp.int32, (16, CH), 0)
     outer_mask = jnp.logical_and(takes_outer, edge_place % 2 == 1 - w)
 
-    def input_stack(stack, source, landing, landing_out, apply):
+    def input_stack(stack, source, landing, landing_out, apply, start):
         def step(f, _):
             edges = []
             for d in range(3):
@@ -330,7 +335,7 @@
                 )
             return 0
 
-        lax.fori_loop(0, frames, step, 0)
+        lax.fori_loop(start, start + fl, step, 0)
 
     def window(stack, f):
         return [stack[f, kr : kr + rl].reshape(cells, 3 * CH) for kr in range(3)]
@@ -501,9 +506,11 @@
         pre = (value - mean1) * factor1 * gain1 + shift1
         return rounded(pre * sigmoid(pre))
 
-    wait_inputs(0, xr, xeb, xex)
-    input_stack(s1, xr, xeb, xex, act_first)
-    convolve(s1, wf1, hid)
+    for dz in near_first:
+        wait_pair(0, dz, xr, xeb, xex)
+        start = pair_from(dz)
+        input_stack(s1, xr, xeb, xex, act_first, start)
+        convolve(s1, wf1, hid, start, start + fl)
 
     def hid_sum(n, total):
         return total + fold_rows(hid[n])
@@ -516,9 +523,11 @@
 
     red_start(1, mean_l, group_sum(total_row(lax.fori_loop(0, frames, hid_spread, zero8))))
 
-    wait_inputs(1, cr, ceb, cex)
-    input_stack(sc, cr, ceb, cex, lambda value: value)
-    convolve(sc, wb2, g2)
+    for dz in near_first:
+        wait_pair(1, dz, cr, ceb, cex)
+        start = pair_from(dz)
+        input_stack(sc, cr, ceb, cex, lambda value: value, start)
+        convolve(sc, wb2, g2, start, start + fl)
     mean2, spread2 = moments_end(1)
     inv2 = 1.0 / jnp.sqrt(spread2 / total_size + EPS)
 
@@ -589,9 +598,12 @@
                 a[0, kr, :, (2 - j) * 3 + kc] = part.reshape(16, 8, CH)
         core_start(0, kr)
 
-    for kr in range(3):
-        put_first(kr)
-    each(a1_start, 0)
+    put_first(0)
+    put_first(1)
+    a1_start(0, 0)
+    put_first(2)
+    a1_start(0, 1)
+    a1_start(0, 2)
     take(hg.at[:, pl.ds(0, 2)], halo_recv.at[0])
     take(heb, halo_recv.at[1])
 
@@ -643,9 +655,9 @@
         send_back(q)
         if q == nz // 2 - 1:
             each(a2_start, 0)
+            each(a3_start, 1)
     t1, t2 = totals
     red_start(3, group_sum(total_row(t1)), group_sum(total_row(t2)))
-    each(a3_start, 1)
     each(a3_start, 0)
     each(g2_start, 1)
     each(g2_start, 0)
@@ -686,6 +698,20 @@
         out_copy(f).wait()
     store_copy(0).wait()
     store_copy(1).wait()
+
+
+def copy_body(*refs):
+    sources, targets, held = refs[0:3], refs[3:6], refs[6:9]
+    load_sem, store_sem = refs[9:]
+    loads = [pltpu.make_async_copy(sources[n], held[n], load_sem.at[n]) for n in range(3)]
+    stores = [pltpu.make_async_copy(held[n], targets[n], store_sem.at[n]) for n in range(3)]
+    for copy in loads:
+        copy.start()
+    for n in range(3):
+        loads[n].wait()
+        stores[n].start()
+    for copy in stores:
+        copy.wait()
 
 
 def shards(sizes, latent, exponents, cotangent, conv_first, conv_second, gain_first, shift_first, gain_second, shift_second):
@@ -751,7 +777,7 @@
         pltpu.SemaphoreType.DMA((4,)),
         pltpu.SemaphoreType.DMA((3,)),
         pltpu.SemaphoreType.DMA((2,)),
-        pltpu.SemaphoreType.DMA((2, 3)),
+        pltpu.SemaphoreType.DMA((2, 3 * nz)),
         pltpu.SemaphoreType.DMA((4,)),
         pltpu.SemaphoreType.DMA((4,)),
         pltpu.SemaphoreType.DMA((1,)),
@@ -761,7 +787,7 @@
         pltpu.SemaphoreType.DMA((2,)),
         pltpu.SemaphoreType.DMA((2, 3, 7)),
     ]
-    return pl.pallas_call(
+    results = pl.pallas_call(
         functools.partial(body, sizes),
         out_shape=(
             jax.ShapeDtypeStruct((CH, fl, rl, cols), F32),
@@ -778,6 +804,15 @@
         latent, cotangent, conv_first, conv_second, exponents[None],
         gain_first[None], shift_first[None], gain_second[None], shift_second[None],
     )
+    return pl.pallas_call(
+        copy_body,
+        out_shape=[jax.ShapeDtypeStruct(value.shape, F32) for value in results],
+        in_specs=[any_space] * 3,
+        out_specs=[any_space] * 3,
+        scratch_shapes=[pltpu.VMEM(value.shape, F32) for value in results]
+        + [pltpu.SemaphoreType.DMA((3,)), pltpu.SemaphoreType.DMA((3,))],
+        compiler_params=pltpu.CompilerParams(vmem_limit_bytes=60 * 1024 * 1024),
+    )(*results)
 
 
 def solution(mesh):

time: 97.3 us -> 94.7 us (0.973)
  local copies, waits for them, and re-layouts: 5.77 us -> 0 us
  Pallas kernels: 90.7 us -> 93.8 us
    unnamed x7 -> x0, local copies, waits for them, and re-layouts: 5.77 us -> none
    pallas_call x0 -> x1, Pallas kernels: none -> 3.95 us  [shards(): pl.pallas_call(copy_body, out_shape=[jax.ShapeDtypeStruct(value.shape, F3...]
where the time goes in v4:
time: 94.7 us; the launch traced here: 94.6 us
  Pallas kernels  93.8 us (99%)
    pallas_call x1, Pallas kernels, shards(): pl.pallas_call(functools.partial(body, sizes), out_shape=(jax.ShapeDtypeS...  89.8 us
    pallas_call x1, Pallas kernels, shards(): pl.pallas_call(copy_body, out_shape=[jax.ShapeDtypeStruct(value.shape, F3...  3.95 us

profile of v4, /device:TPU:1, one launch (start us, length us, event | category | flops | bytes accessed | tf_op | source)
XLA Modules:
  0.0 94.6 jit_solution(4201450347340327708)
XLA Ops:
  0.6 89.8 %shard_map.112 = (f32[128,2,4,256]{3,2,1,0:T(4,128)}, f32[128,3456]{1,0:T(8,128)}, f32[128,3456]{1,0:T(8,128)}) custom-call(bf16[128,2,4,256]{3,2,1,0:T(4,128)(2,1)} %x_hbm.1, bf16[128,2,4,256]{3,2,1,0:T(4,128)(2,1)} %c_hbm.1, bf16[128,3456]{1,0:T(8,128)(2,1)} %w1_hbm.1, bf16[128,3456]{1,0:T(8,128)(2,1)} %w2_hbm.1, s32[1,32]{1,0:T(1,128)} %bitcast.5, ...), custom_call_target="tpu_custom_call" | custom-call | tf_op jit(solution)/shard_map/pallas_call | solution.py:790
  90.5 3.9 %shard_map.113 = (f32[128,2,4,256]{3,2,1,0:T(4,128)}, f32[128,3456]{1,0:T(8,128)}, f32[128,3456]{1,0:T(8,128)}) custom-call(f32[128,2,4,256]{3,2,1,0:T(4,128)} %get-tuple-element.6.refs_0_, f32[128,3456]{1,0:T(8,128)} %get-tuple-element.7.refs_1_, f32[128,3456]{1,0:T(8,128)} %get-tuple-element.8.refs_2_), custom_call_target="tpu_custom_call" | custom-call | tf_op jit(solution)/shard_map/pallas_call | solution.py:807

commit v5 on v4

--- a/solution.py
+++ b/solution.py
@@ -116,20 +116,21 @@
         )
 
     own_frames = pl.ds(z * fl, fl)
-    row_parts = {0: ((0, rl), (1, rl)), 1: ((rl - 1, 1), (0, 1)), -1: ((0, 1), (rl + 1, 1))}
-
-    def main_copies(k, src, dst):
+
+    def strip_copies(k, src, dst, edges, landing):
         copies = []
-        for dz in range(nz):
+        for dz in sorted(range(nz), key=lambda dz: -min(dz, nz - dz)):
             q = lax.rem(z + dz, nz)
-            for n, dh in enumerate((0, 1, -1)):
-                (r_from, count), (r_to, _) = row_parts[dh]
-                source = src.at[:, pl.ds(r_from, count), pl.ds(pl.multiple_of(q * strip, strip), strip), :]
-                target = dst.at[own_frames, pl.ds(r_to, count)]
-                if dz == 0 and dh == 0:
-                    copies.append(pltpu.make_async_copy(source, target, in_recv.at[k, 0]))
+            pieces = (
+                (src.at[:, :, pl.ds(pl.multiple_of(q * strip, strip), strip), :],
+                 dst.at[own_frames, pl.ds(1, rl)], in_recv.at[k, dz]),
+                (edges.at[q], landing.at[1, own_frames], in_recv.at[k, nz + dz]),
+            )
+            for source, target, recv in pieces:
+                if dz == 0:
+                    copies.append((False, pltpu.make_async_copy(source, target, recv)))
                 else:
-                    copies.append(remote(source, target, in_send.at[k], in_recv.at[k, dz], dev(dz, dh, 0)))
+                    copies.append((True, remote(source, target, in_send.at[k], recv, dev(dz, 0, 0))))
         return copies
 
     def build_edges(src, edges):
@@ -153,43 +154,76 @@
                 tile = jnp.where(place // 2 == r, outer, tile)
             edges[nz, f] = tile.astype(BF16)
 
-    def edge_copies(k, edges, landing, landing_out):
-        copies = []
-        for dz in range(nz):
-            q = lax.rem(z + dz, nz)
-            for n, dh in enumerate((0, 1, -1)):
-                source = edges.at[q]
-                target = landing.at[1 - dh, own_frames]
-                if dz == 0 and dh == 0:
-                    copies.append(pltpu.make_async_copy(source, target, in_recv.at[k, nz]))
-                else:
-                    copies.append(remote(source, target, in_send.at[k], in_recv.at[k, nz + dz], dev(dz, dh, 0)))
-        return copies
-
     outer_q = (nz - 1) * w
     takes_outer = z == (nz - 1) * (1 - w)
 
-    def outer_sends(k, edges, landing_out):
-        copies = []
+    def outer_copy(k, edges, landing_out):
         recv = in_recv.at[k, 2 * nz + lax.rem(outer_q - z + nz, nz)]
-        for dh in (0, 1, -1):
-            where = (outer_q, lax.rem(h + dh + nh, nh), 1 - w)
-            copies.append(remote(edges.at[nz], landing_out.at[1 - dh, own_frames], in_send.at[k], recv, where))
-        return copies
+        return remote(edges.at[nz], landing_out.at[1, own_frames], in_send.at[k], recv, (outer_q, h, 1 - w))
+
+    def start_inputs(k, src, dst, edges, landing, landing_out):
+        copies = strip_copies(k, src, dst, edges, landing)
+        for _, copy in copies:
+            copy.start()
+        outer = outer_copy(k, edges, landing_out)
+        outer.start()
+        return [copy for far, copy in copies if far] + [outer]
 
     near_first = sorted(range(nz), key=lambda dz: min(dz, nz - dz))
 
     def pair_from(dz):
         return lax.rem(z - dz + nz, nz) * fl
 
+    def beside_copies(k, dz, cells_in, landing):
+        pair = pl.ds(pair_from(dz), fl)
+        copies = []
+        for dh, r_from, r_to in ((1, rl, 0), (-1, 1, rl + 1)):
+            where = dev(0, dh, 0)
+            copies.append(
+                remote(cells_in.at[pair, pl.ds(r_from, 1)], cells_in.at[pair, pl.ds(r_to, 1)],
+                       in_send.at[k], in_recv.at[k, 3 * nz + dz], where)
+            )
+            copies.append(
+                remote(landing.at[1, pair], landing.at[1 - dh, pair], in_send.at[k], in_recv.at[k, 4 * nz + dz], where)
+            )
+        return copies
+
+    def beside_outer(k, dz, landing_out):
+        pair = pl.ds(pair_from(dz), fl)
+        return [
+            remote(landing_out.at[1, pair], landing_out.at[1 - dh, pair],
+                   in_send.at[k], in_recv.at[k, 5 * nz + dz], dev(0, dh, 0))
+            for dh in (1, -1)
+        ]
+
+    def hand_on(k, dz, cells_in, landing, landing_out):
+        pair = pl.ds(pair_from(dz), fl)
+        take(cells_in.at[pair, pl.ds(1, rl)], in_recv.at[k, dz])
+        take(landing.at[1, pair], in_recv.at[k, nz + dz])
+        start_all(beside_copies(k, dz, cells_in, landing))
+
+        @pl.when(takes_outer)
+        def _():
+            take(landing_out.at[1, pair], in_recv.at[k, 2 * nz + dz])
+            start_all(beside_outer(k, dz, landing_out))
+
     def wait_pair(k, dz, cells_in, landing, landing_out):
         pair = pl.ds(pair_from(dz), fl)
-        take(cells_in.at[pair], in_recv.at[k, dz])
-        take(landing.at[:, pair], in_recv.at[k, nz + dz])
+        take(cells_in.at[pair, pl.ds(0, 2)], in_recv.at[k, 3 * nz + dz])
+        take(landing.at[pl.ds(0, 2), pair], in_recv.at[k, 4 * nz + dz])
 
         @pl.when(takes_outer)
         def _():
-            take(landing_out.at[:, pair], in_recv.at[k, 2 * nz + dz])
+            take(landing_out.at[pl.ds(0, 2), pair], in_recv.at[k, 5 * nz + dz])
+
+    def close_inputs(k, sent, cells_in, landing, landing_out):
+        wait_sends(sent)
+        for dz in range(nz):
+            wait_sends(beside_copies(k, dz, cells_in, landing))
+
+            @pl.when(takes_outer)
+            def _():
+                wait_sends(beside_outer(k, dz, landing_out))
 
     def start_all(copies):
         for copy in copies:
@@ -265,15 +299,9 @@
                 block = w1[:, tap * CH : (tap + 1) * CH].astype(F32)
                 wf1[ahead : ahead + CH, (2 - kt) * CH : (3 - kt) * CH] = jnp.transpose(block).astype(BF16)
     pl.semaphore_wait(barrier, devices - 1)
-    x_main = main_copies(0, xl, xr)
-    x_edge = edge_copies(0, xe, xeb, xex)
-    x_outer = outer_sends(0, xe, xex)
-    start_all(x_main + x_edge + x_outer)
+    x_sent = start_inputs(0, xl, xr, xe, xeb, xex)
     red_start(0, local_mean, local_spread)
-    c_main = main_copies(1, cl, cr)
-    c_edge = edge_copies(1, ce, ceb, cex)
-    c_outer = outer_sends(1, ce, cex)
-    start_all(c_main + c_edge + c_outer)
+    c_sent = start_inputs(1, cl, cr, ce, ceb, cex)
     zero_cells = jnp.zeros((cells, CH), F32)
 
     def clear(n, _):
@@ -488,6 +516,8 @@
         for p in range(3):
             stage(g, p)
 
+    for dz in near_first:
+        hand_on(0, dz, xr, xeb, xex)
     mean1, spread1 = moments_end(0)
     picks = lax.broadcasted_iota(jnp.int32, (CH // 4, CH), 1) // 4 == lax.broadcasted_iota(jnp.int32, (CH // 4, CH), 0)
     spread_exponent = jnp.dot(
@@ -511,6 +541,7 @@
         start = pair_from(dz)
         input_stack(s1, xr, xeb, xex, act_first, start)
         convolve(s1, wf1, hid, start, start + fl)
+        hand_on(1, dz, cr, ceb, cex)
 
     def hid_sum(n, total):
         return total + fold_rows(hid[n])
@@ -604,6 +635,7 @@
     put_first(2)
     a1_start(0, 1)
     a1_start(0, 2)
+    each(a2_start, 1)
     take(hg.at[:, pl.ds(0, 2)], halo_recv.at[0])
     take(heb, halo_recv.at[1])
 
@@ -616,7 +648,6 @@
         return 0
 
     lax.fori_loop(0, frames, halo_stack, 0)
-    each(a2_start, 1)
 
     def first(f, totals):
         first_total, second_total = totals
@@ -647,6 +678,8 @@
             far.start()
 
     convolve(sh, wb1, g1, 0, 2)
+    each(a2_start, 0)
+    each(a3_start, 1)
     totals = (zero8, zero8)
     for q in range(nz):
         if q * fl + 2 < frames:
@@ -654,14 +687,13 @@
         totals = lax.fori_loop(q * fl, q * fl + fl, first, totals)
         send_back(q)
         if q == nz // 2 - 1:
-            each(a2_start, 0)
-            each(a3_start, 1)
+            each(a3_start, 0)
+            each(g2_start, 1)
     t1, t2 = totals
     red_start(3, group_sum(total_row(t1)), group_sum(total_row(t2)))
-    each(a3_start, 0)
-    each(g2_start, 1)
     each(g2_start, 0)
     each(g1_start, 1)
+    each(g1_start, 0)
     m1, m2 = sums_end(3)
     take(s_in, back_recv.at[0])
 
@@ -674,12 +706,11 @@
             value = cl[f, r].astype(F32) + inv1 * (s_in[f, r].astype(F32) - m1 - normed * m2)
             out_ref[:, f, r, :] = jnp.transpose(value)
         out_copy(f).start()
-    each(g1_start, 0)
     each(gc_start, 1)
     each(gc_end, 1)
     store_copy(1).start()
-    wait_sends(x_main[1:] + x_edge[1:] + x_outer)
-    wait_sends(c_main[1:] + c_edge[1:] + c_outer)
+    close_inputs(0, x_sent, xr, xeb, xex)
+    close_inputs(1, c_sent, cr, ceb, cex)
     for k in range(4):
         take(rb.at[k, pl.ds(0, devices - 1)], red_send.at[k])
     wait_sends(halo)
@@ -777,7 +808,7 @@
         pltpu.SemaphoreType.DMA((4,)),
         pltpu.SemaphoreType.DMA((3,)),
         pltpu.SemaphoreType.DMA((2,)),
-        pltpu.SemaphoreType.DMA((2, 3 * nz)),
+        pltpu.SemaphoreType.DMA((2, 6 * nz)),
         pltpu.SemaphoreType.DMA((4,)),
         pltpu.SemaphoreType.DMA((4,)),
         pltpu.SemaphoreType.DMA((1,)),

time: 94.7 us -> 88.3 us (0.932)
  Pallas kernels: 93.8 us -> 87.3 us
    pallas_call x1, Pallas kernels: 89.8 us -> 83.4 us  [shards(): pl.pallas_call(functools.partial(body, sizes), out_shape=(jax.ShapeDtypeS...]
where the time goes in v5:
time: 88.3 us; the launch traced here: 88.1 us
  Pallas kernels  87.3 us (99%)
    pallas_call x1, Pallas kernels, shards(): pl.pallas_call(functools.partial(body, sizes), out_shape=(jax.ShapeDtypeS...  83.4 us
    pallas_call x1, Pallas kernels, shards(): pl.pallas_call(copy_body, out_shape=[jax.ShapeDtypeStruct(value.shape, F3...  3.95 us

profile of v5, /device:TPU:1, one launch (start us, length us, event | category | flops | bytes accessed | tf_op | source)
XLA Modules:
  0.0 88.1 jit_solution(10624111188894191230)
XLA Ops:
  0.6 83.4 %shard_map.112 = (f32[128,2,4,256]{3,2,1,0:T(4,128)}, f32[128,3456]{1,0:T(8,128)}, f32[128,3456]{1,0:T(8,128)}) custom-call(bf16[128,2,4,256]{3,2,1,0:T(4,128)(2,1)} %x_hbm.1, bf16[128,2,4,256]{3,2,1,0:T(4,128)(2,1)} %c_hbm.1, bf16[128,3456]{1,0:T(8,128)(2,1)} %w1_hbm.1, bf16[128,3456]{1,0:T(8,128)(2,1)} %w2_hbm.1, s32[1,32]{1,0:T(1,128)} %bitcast.5, ...), custom_call_target="tpu_custom_call" | custom-call | tf_op jit(solution)/shard_map/pallas_call | solution.py:821
  84.0 3.9 %shard_map.113 = (f32[128,2,4,256]{3,2,1,0:T(4,128)}, f32[128,3456]{1,0:T(8,128)}, f32[128,3456]{1,0:T(8,128)}) custom-call(f32[128,2,4,256]{3,2,1,0:T(4,128)} %get-tuple-element.6.refs_0_, f32[128,3456]{1,0:T(8,128)} %get-tuple-element.7.refs_1_, f32[128,3456]{1,0:T(8,128)} %get-tuple-element.8.refs_2_), custom_call_target="tpu_custom_call" | custom-call | tf_op jit(solution)/shard_map/pallas_call | solution.py:838

commit v6 on v5

--- a/solution.py
+++ b/solution.py
@@ -54,11 +54,11 @@
 def body(
     sizes,
     x_hbm, c_hbm, w1_hbm, w2_hbm, exponent_ref, gain1_ref, shift1_ref, gain2_ref, shift2_ref,
-    out_hbm, o1_hbm, o2_hbm,
-    x_raw, c_raw, xl, cl, w1, w2, out_ref, o1_ref, o2_ref, fin1, fin2,
+    out_ref, fin1, fin2,
+    x_raw, c_raw, xl, cl, w1, w2, o1_ref, o2_ref,
     xr, cr, xe, ce, xeb, ceb, xex, cex, s1, sc, sh, hid, g2, g1, nrm, act_t, hg_t, hg, eh, heb,
     wf1, wb1, wb2, s_out, s_in, rb, a, r0, b1, r1, b2, r2, r3, g3,
-    load_sem, store_sem, in_send, in_recv, red_send, red_recv, halo_send, halo_recv, back_send, back_recv,
+    load_sem, in_send, in_recv, red_send, red_recv, halo_send, halo_recv, back_send, back_recv,
     ar_send, ar_recv,
 ):
     nz, nh, nx, ny = sizes
@@ -300,6 +300,7 @@
                 wf1[ahead : ahead + CH, (2 - kt) * CH : (3 - kt) * CH] = jnp.transpose(block).astype(BF16)
     pl.semaphore_wait(barrier, devices - 1)
     x_sent = start_inputs(0, xl, xr, xe, xeb, xex)
+    hand_on(0, 0, xr, xeb, xex)
     red_start(0, local_mean, local_spread)
     c_sent = start_inputs(1, cl, cr, ce, ceb, cex)
     zero_cells = jnp.zeros((cells, CH), F32)
@@ -496,9 +497,6 @@
         for j in range(1, ns):
             gc_copy(g, p, j).start()
 
-    def store_copy(g):
-        return pltpu.make_async_copy((fin1, fin2)[g], (o1_hbm, o2_hbm)[g], store_sem.at[1 + g])
-
     def gc_end(g, p):
         arrived(g, p, "gc", outs[g].at[p, pl.ds(0, half)])
         for kt in range(3):
@@ -516,8 +514,9 @@
         for p in range(3):
             stage(g, p)
 
-    for dz in near_first:
+    for dz in near_first[1:]:
         hand_on(0, dz, xr, xeb, xex)
+    hand_on(1, 0, cr, ceb, cex)
     mean1, spread1 = moments_end(0)
     picks = lax.broadcasted_iota(jnp.int32, (CH // 4, CH), 1) // 4 == lax.broadcasted_iota(jnp.int32, (CH // 4, CH), 0)
     spread_exponent = jnp.dot(
@@ -536,12 +535,13 @@
         pre = (value - mean1) * factor1 * gain1 + shift1
         return rounded(pre * sigmoid(pre))
 
-    for dz in near_first:
+    for n, dz in enumerate(near_first):
         wait_pair(0, dz, xr, xeb, xex)
         start = pair_from(dz)
         input_stack(s1, xr, xeb, xex, act_first, start)
         convolve(s1, wf1, hid, start, start + fl)
-        hand_on(1, dz, cr, ceb, cex)
+        for later in (near_first[1:-1], near_first[-1:], [])[min(n, 2)]:
+            hand_on(1, later, cr, ceb, cex)
 
     def hid_sum(n, total):
         return total + fold_rows(hid[n])
@@ -586,7 +586,6 @@
 
     for kr in range(3):
         put_second(kr)
-    each(a1_start, 1)
     m1, m2 = sums_end(2)
 
     def hidden(n, _):
@@ -620,6 +619,7 @@
         halo.append(remote(eh.at[0], heb.at[1 - dh, 1], halo_send.at[0], halo_recv.at[1], beside(-1, dh)))
         halo.append(remote(eh.at[1], heb.at[1 - dh, 0], halo_send.at[0], halo_recv.at[1], beside(1, dh)))
     start_all(halo)
+    each(a1_start, 1)
 
     def put_first(kr):
         block = weight_part(hg_t, s1, kr)
@@ -697,18 +697,13 @@
     m1, m2 = sums_end(3)
     take(s_in, back_recv.at[0])
 
-    def out_copy(f):
-        return pltpu.make_async_copy(out_ref.at[:, f], out_hbm.at[:, f], store_sem.at[0])
-
     for f in range(fl):
         for r in range(rl):
             normed = (xl[f, r].astype(F32) - mean1) * factor1
             value = cl[f, r].astype(F32) + inv1 * (s_in[f, r].astype(F32) - m1 - normed * m2)
             out_ref[:, f, r, :] = jnp.transpose(value)
-        out_copy(f).start()
     each(gc_start, 1)
     each(gc_end, 1)
-    store_copy(1).start()
     close_inputs(0, x_sent, xr, xeb, xex)
     close_inputs(1, c_sent, cr, ceb, cex)
     for k in range(4):
@@ -723,24 +718,14 @@
     ar_close(1)
     each(gc_start, 0)
     each(gc_end, 0)
-    store_copy(0).start()
     ar_close(0)
-    for f in range(fl):
-        out_copy(f).wait()
-    store_copy(0).wait()
-    store_copy(1).wait()
 
 
 def copy_body(*refs):
-    sources, targets, held = refs[0:3], refs[3:6], refs[6:9]
-    load_sem, store_sem = refs[9:]
-    loads = [pltpu.make_async_copy(sources[n], held[n], load_sem.at[n]) for n in range(3)]
-    stores = [pltpu.make_async_copy(held[n], targets[n], store_sem.at[n]) for n in range(3)]
-    for copy in loads:
+    sources, targets, store_sem = refs[0:3], refs[3:6], refs[6]
+    stores = [pltpu.make_async_copy(sources[n], targets[n], store_sem.at[n]) for n in range(3)]
+    for copy in stores:
         copy.start()
-    for n in range(3):
-        loads[n].wait()
-        stores[n].start()
     for copy in stores:
         copy.wait()
 
@@ -766,11 +751,8 @@
         pltpu.VMEM((fl, rl, cols, CH), BF16),
         pltpu.VMEM((CH, 27 * CH), BF16),
         pltpu.VMEM((CH, 27 * CH), BF16),
-        pltpu.VMEM((CH, fl, rl, cols), F32),
         pltpu.VMEM(part, F32),
         pltpu.VMEM(part, F32),
-        pltpu.VMEM((CH, 27 * CH), F32),
-        pltpu.VMEM((CH, 27 * CH), F32),
         pltpu.VMEM((frames, rl + 2, strip, CH), BF16),
         pltpu.VMEM((frames, rl + 2, strip, CH), BF16),
         pltpu.VMEM((nz + 1, fl, 16, CH), BF16),
@@ -806,7 +788,6 @@
         pltpu.VMEM((2, 3, ns, piece, 8, CH), F32),
         pltpu.VMEM((2, 3, piece * ns, 8, CH), F32),
         pltpu.SemaphoreType.DMA((4,)),
-        pltpu.SemaphoreType.DMA((3,)),
         pltpu.SemaphoreType.DMA((2,)),
         pltpu.SemaphoreType.DMA((2, 6 * nz)),
         pltpu.SemaphoreType.DMA((4,)),
@@ -821,15 +802,15 @@
     results = pl.pallas_call(
         functools.partial(body, sizes),
         out_shape=(
-            jax.ShapeDtypeStruct((CH, fl, rl, cols), F32),
-            jax.ShapeDtypeStruct((CH, 27 * CH), F32),
-            jax.ShapeDtypeStruct((CH, 27 * CH), F32),
+            pltpu.VMEM((CH, fl, rl, cols), F32),
+            pltpu.VMEM((CH, 27 * CH), F32),
+            pltpu.VMEM((CH, 27 * CH), F32),
         ),
         in_specs=[any_space] * 4 + [vmem] * 5,
-        out_specs=(any_space,) * 3,
+        out_specs=(vmem,) * 3,
         scratch_shapes=scratch,
         compiler_params=pltpu.CompilerParams(
-            collective_id=0, has_side_effects=True, vmem_limit_bytes=60 * 1024 * 1024
+            collective_id=0, has_side_effects=True, vmem_limit_bytes=48 * 1024 * 1024
         ),
     )(
         latent, cotangent, conv_first, conv_second, exponents[None],
@@ -838,11 +819,10 @@
     return pl.pallas_call(
         copy_body,
         out_shape=[jax.ShapeDtypeStruct(value.shape, F32) for value in results],
-        in_specs=[any_space] * 3,
+        in_specs=[vmem] * 3,
         out_specs=[any_space] * 3,
-        scratch_shapes=[pltpu.VMEM(value.shape, F32) for value in results]
-        + [pltpu.SemaphoreType.DMA((3,)), pltpu.SemaphoreType.DMA((3,))],
-        compiler_params=pltpu.CompilerParams(vmem_limit_bytes=60 * 1024 * 1024),
+        scratch_shapes=[pltpu.SemaphoreType.DMA((3,))],
+        compiler_params=pltpu.CompilerParams(vmem_limit_bytes=8 * 1024 * 1024),
     )(*results)
 
 

time: 88.3 us -> 91.7 us (1.039)
  local copies, waits for them, and re-layouts: 0 us -> 5.35 us
  Pallas kernels: 87.3 us -> 85.3 us
    unnamed x0 -> x14, local copies, waits for them, and re-layouts: none -> 5.35 us
    pallas_call x1, Pallas kernels: 3.95 us -> 2.16 us  [shards(): pl.pallas_call(copy_body, out_shape=[jax.ShapeDtypeStruct(value.shape, F3...]
where the time goes in v6:
time: 91.7 us; the launch traced here: 91.4 us
  Pallas kernels  85.3 us (93%)
  local copies, waits for them, and re-layouts  5.35 us (6%)
    pallas_call x1, Pallas kernels, shards(): pl.pallas_call(functools.partial(body, sizes), out_shape=(pltpu.VMEM((CH,...  83.1 us
    unnamed x14, local copies, waits for them, and re-layouts  5.35 us
    pallas_call x1, Pallas kernels, shards(): pl.pallas_call(copy_body, out_shape=[jax.ShapeDtypeStruct(value.shape, F3...  2.16 us

profile of v6, /device:TPU:1, one launch (start us, length us, event | category | flops | bytes accessed | tf_op | source)
XLA Modules:
  0.0 91.4 jit_solution(5082904380023130985)
XLA Ops:
  0.6 0.0 copy-start
  0.6 1.0 %copy-done = bf16[128,2,4,256]{3,2,1,0:T(4,128)(2,1)S(1)} copy-done((bf16[128,2,4,256]{3,2,1,0:T(4,128)(2,1)S(1)}, bf16[128,2,4,256]{3,2,1,0:T(4,128)(2,1)}, u32[]{:S(2)}) %copy-start) | copy-done | bytes 524312
  1.7 0.0 copy-start.1
  1.7 1.0 %copy-done.1 = bf16[128,2,4,256]{3,2,1,0:T(4,128)(2,1)S(1)} copy-done((bf16[128,2,4,256]{3,2,1,0:T(4,128)(2,1)S(1)}, bf16[128,2,4,256]{3,2,1,0:T(4,128)(2,1)}, u32[]{:S(2)}) %copy-start.1) | copy-done | bytes 524312
  2.7 0.0 copy-start.2
  2.7 0.7 copy-done.2
  3.4 0.0 copy-start.3
  3.4 0.7 copy-done.3
  4.0 0.0 copy-start.4
  4.0 0.7 copy-done.4
  4.7 0.0 copy-start.5
  4.7 0.7 copy-done.5
  5.3 0.0 copy-start.6
  5.3 0.7 copy-done.6
  6.0 83.1 %shard_map.112 = (f32[128,2,4,256]{3,2,1,0:T(4,128)S(1)}, f32[128,3456]{1,0:T(8,128)S(1)}, f32[128,3456]{1,0:T(8,128)S(1)}) custom-call(bf16[128,2,4,256]{3,2,1,0:T(4,128)(2,1)S(1)} %copy-done, bf16[128,2,4,256]{3,2,1,0:T(4,128)(2,1)S(1)} %copy-done.1, bf16[128,3456]{1,0:T(8,128)(2,1)} %w1_hbm.1, bf16[128,3456]{1,0:T(8,128)(2,1)} %w2_hbm.1, ...), custom_call_target="tpu_custom_call" | custom-call | tf_op jit(solution)/shard_map/pallas_call | solution.py:802
  89.1 2.2 %shard_map.113 = (f32[128,2,4,256]{3,2,1,0:T(4,128)}, f32[128,3456]{1,0:T(8,128)}, f32[128,3456]{1,0:T(8,128)}) custom-call(f32[128,2,4,256]{3,2,1,0:T(4,128)S(1)} %get-tuple-element.6.refs_0_, f32[128,3456]{1,0:T(8,128)S(1)} %get-tuple-element.7.refs_1_, f32[128,3456]{1,0:T(8,128)S(1)} %get-tuple-element.8.refs_2_), custom_call_target="tpu_custom_call" | custom-call | tf_op jit(solution)/shard_map/pallas_call | solution.py:819
Async XLA Ops:
  0.6 1.0 %copy-start = (bf16[128,2,4,256]{3,2,1,0:T(4,128)(2,1)S(1)}, bf16[128,2,4,256]{3,2,1,0:T(4,128)(2,1)}, u32[]{:S(2)}) copy-start(bf16[128,2,4,256]{3,2,1,0:T(4,128)(2,1)} %x_hbm.1) | copy-start | bytes 1572868
  1.7 1.0 %copy-start.1 = (bf16[128,2,4,256]{3,2,1,0:T(4,128)(2,1)S(1)}, bf16[128,2,4,256]{3,2,1,0:T(4,128)(2,1)}, u32[]{:S(2)}) copy-start(bf16[128,2,4,256]{3,2,1,0:T(4,128)(2,1)} %c_hbm.1) | copy-start | bytes 1572868
  2.7 0.7 copy-start.2
  3.4 0.7 copy-start.3
  4.0 0.7 copy-start.4
  4.7 0.7 copy-start.5
  5.3 0.7 copy-start.6

commit v7 on v6

--- a/solution.py
+++ b/solution.py
@@ -300,9 +300,9 @@
                 wf1[ahead : ahead + CH, (2 - kt) * CH : (3 - kt) * CH] = jnp.transpose(block).astype(BF16)
     pl.semaphore_wait(barrier, devices - 1)
     x_sent = start_inputs(0, xl, xr, xe, xeb, xex)
-    hand_on(0, 0, xr, xeb, xex)
     red_start(0, local_mean, local_spread)
     c_sent = start_inputs(1, cl, cr, ce, ceb, cex)
+    hand_on(0, 0, xr, xeb, xex)
     zero_cells = jnp.zeros((cells, CH), F32)
 
     def clear(n, _):
@@ -516,7 +516,6 @@
 
     for dz in near_first[1:]:
         hand_on(0, dz, xr, xeb, xex)
-    hand_on(1, 0, cr, ceb, cex)
     mean1, spread1 = moments_end(0)
     picks = lax.broadcasted_iota(jnp.int32, (CH // 4, CH), 1) // 4 == lax.broadcasted_iota(jnp.int32, (CH // 4, CH), 0)
     spread_exponent = jnp.dot(
@@ -540,8 +539,7 @@
         start = pair_from(dz)
         input_stack(s1, xr, xeb, xex, act_first, start)
         convolve(s1, wf1, hid, start, start + fl)
-        for later in (near_first[1:-1], near_first[-1:], [])[min(n, 2)]:
-            hand_on(1, later, cr, ceb, cex)
+        hand_on(1, dz, cr, ceb, cex)
 
     def hid_sum(n, total):
         return total + fold_rows(hid[n])
@@ -586,6 +584,7 @@
 
     for kr in range(3):
         put_second(kr)
+    each(a1_start, 1)
     m1, m2 = sums_end(2)
 
     def hidden(n, _):
@@ -619,7 +618,6 @@
         halo.append(remote(eh.at[0], heb.at[1 - dh, 1], halo_send.at[0], halo_recv.at[1], beside(-1, dh)))
         halo.append(remote(eh.at[1], heb.at[1 - dh, 0], halo_send.at[0], halo_recv.at[1], beside(1, dh)))
     start_all(halo)
-    each(a1_start, 1)
 
     def put_first(kr):
         block = weight_part(hg_t, s1, kr)
@@ -810,7 +808,7 @@
         out_specs=(vmem,) * 3,
         scratch_shapes=scratch,
         compiler_params=pltpu.CompilerParams(
-            collective_id=0, has_side_effects=True, vmem_limit_bytes=48 * 1024 * 1024
+            collective_id=0, has_side_effects=True, vmem_limit_bytes=58 * 1024 * 1024
         ),
     )(
         latent, cotangent, conv_first, conv_second, exponents[None],

time: 91.7 us -> 85.2 us (0.929)
  local copies, waits for them, and re-layouts: 5.35 us -> 0 us
  Pallas kernels: 85.3 us -> 84.3 us
    unnamed x14 -> x0, local copies, waits for them, and re-layouts: 5.35 us -> none
    pallas_call x1, Pallas kernels: 83.1 us -> 82.1 us  [shards(): pl.pallas_call(functools.partial(body, sizes), out_shape=(pltpu.VMEM((CH,...]
where the time goes in v7:
time: 85.2 us; the launch traced here: 85.1 us
  Pallas kernels  84.3 us (99%)
    pallas_call x1, Pallas kernels, shards(): pl.pallas_call(functools.partial(body, sizes), out_shape=(pltpu.VMEM((CH,...  82.1 us
    pallas_call x1, Pallas kernels, shards(): pl.pallas_call(copy_body, out_shape=[jax.ShapeDtypeStruct(value.shape, F3...  2.16 us

profile of v7, /device:TPU:1, one launch (start us, length us, event | category | flops | bytes accessed | tf_op | source)
XLA Modules:
  0.0 85.1 jit_solution(53680572067087503)
XLA Ops:
  0.6 82.1 %shard_map.112 = (f32[128,2,4,256]{3,2,1,0:T(4,128)S(1)}, f32[128,3456]{1,0:T(8,128)S(1)}, f32[128,3456]{1,0:T(8,128)S(1)}) custom-call(bf16[128,2,4,256]{3,2,1,0:T(4,128)(2,1)} %x_hbm.1, bf16[128,2,4,256]{3,2,1,0:T(4,128)(2,1)} %c_hbm.1, bf16[128,3456]{1,0:T(8,128)(2,1)} %w1_hbm.1, bf16[128,3456]{1,0:T(8,128)(2,1)} %w2_hbm.1, s32[1,32]{1,0:T(1,128)} %bitcast.5, ...), custom_call_target="tpu_custom_call" | custom-call | tf_op jit(solution)/shard_map/pallas_call | solution.py:800
  82.8 2.2 %shard_map.113 = (f32[128,2,4,256]{3,2,1,0:T(4,128)}, f32[128,3456]{1,0:T(8,128)}, f32[128,3456]{1,0:T(8,128)}) custom-call(f32[128,2,4,256]{3,2,1,0:T(4,128)S(1)} %get-tuple-element.6.refs_0_, f32[128,3456]{1,0:T(8,128)S(1)} %get-tuple-element.7.refs_1_, f32[128,3456]{1,0:T(8,128)S(1)} %get-tuple-element.8.refs_2_), custom_call_target="tpu_custom_call" | custom-call | tf_op jit(solution)/shard_map/pallas_call | solution.py:817

commit v8 on v7

--- a/solution.py
+++ b/solution.py
@@ -497,13 +497,23 @@
         for j in range(1, ns):
             gc_copy(g, p, j).start()
 
+    def settle(p, side):
+        rows = pl.ds(pl.multiple_of(side * half * 8, half * 8), half * 8)
+        for kt in range(3):
+            for kc in range(3):
+                tap = 9 * kt + 3 * p + kc
+                block = o1_ref[p, pl.ds(side * half, half), kt * 3 + kc].reshape(half * 8, CH)
+                fin1[rows, tap * CH : (tap + 1) * CH] = block
+
     def gc_end(g, p):
         arrived(g, p, "gc", outs[g].at[p, pl.ds(0, half)])
+        if g == 0:
+            settle(p, 1 - w)
+            return
         for kt in range(3):
             for kc in range(3):
-                block = outs[g][p, :, kt * 3 + kc].reshape(CH, CH)
                 tap = 9 * kt + 3 * p + kc
-                (fin1, fin2)[g][:, tap * CH : (tap + 1) * CH] = block if g == 0 else jnp.transpose(block)
+                fin2[:, tap * CH : (tap + 1) * CH] = jnp.transpose(outs[g][p, :, kt * 3 + kc].reshape(CH, CH))
 
     def ar_close(g):
         for p in range(3):
@@ -715,6 +725,8 @@
 
     ar_close(1)
     each(gc_start, 0)
+    for p in range(3):
+        settle(p, w)
     each(gc_end, 0)
     ar_close(0)
 

time: 85.2 us -> 85.2 us (level)
  no operation moved by 1% of the time
where the time goes in v8:
time: 85.2 us; the launch traced here: 85.1 us
  Pallas kernels  84.3 us (99%)
    pallas_call x1, Pallas kernels, shards(): pl.pallas_call(functools.partial(body, sizes), out_shape=(pltpu.VMEM((CH,...  82.1 us
    pallas_call x1, Pallas kernels, shards(): pl.pallas_call(copy_body, out_shape=[jax.ShapeDtypeStruct(value.shape, F3...  2.16 us

profile of v8, /device:TPU:1, one launch (start us, length us, event | category | flops | bytes accessed | tf_op | source)
XLA Modules:
  0.0 85.1 jit_solution(16890000375103760485)
XLA Ops:
  0.6 82.1 %shard_map.112 = (f32[128,2,4,256]{3,2,1,0:T(4,128)S(1)}, f32[128,3456]{1,0:T(8,128)S(1)}, f32[128,3456]{1,0:T(8,128)S(1)}) custom-call(bf16[128,2,4,256]{3,2,1,0:T(4,128)(2,1)} %x_hbm.1, bf16[128,2,4,256]{3,2,1,0:T(4,128)(2,1)} %c_hbm.1, bf16[128,3456]{1,0:T(8,128)(2,1)} %w1_hbm.1, bf16[128,3456]{1,0:T(8,128)(2,1)} %w2_hbm.1, s32[1,32]{1,0:T(1,128)} %bitcast.5, ...), custom_call_target="tpu_custom_call" | custom-call | tf_op jit(solution)/shard_map/pallas_call | solution.py:812
  82.8 2.2 %shard_map.113 = (f32[128,2,4,256]{3,2,1,0:T(4,128)}, f32[128,3456]{1,0:T(8,128)}, f32[128,3456]{1,0:T(8,128)}) custom-call(f32[128,2,4,256]{3,2,1,0:T(4,128)S(1)} %get-tuple-element.6.refs_0_, f32[128,3456]{1,0:T(8,128)S(1)} %get-tuple-element.7.refs_1_, f32[128,3456]{1,0:T(8,128)S(1)} %get-tuple-element.8.refs_2_), custom_call_target="tpu_custom_call" | custom-call | tf_op jit(solution)/shard_map/pallas_call | solution.py:829
